TPU v7x, 128 devices: a whole 4x4x4 slice. The times are simulated.
128 devices in a mesh: row: 16 (over y_lo, x, core), col: 8 (over y_hi, z).
Axes of the slice: x: 4, y: 4 (y_hi: 2, y_lo: 2; y = y_hi * 2 + y_lo), z: 4, core: 2. Of those that a mesh axis runs over, the one named last changes fastest.
Arguments:
- pair_repr: bfloat16 [896, 896, 128], P('row', 'col'), may hold values from -6 to 6
- residue_mask: int32 [896], replicated, may hold values 0 or 1
- chain_index: int32 [896], replicated, may hold values from 0 to 3, never falling along the last dimension, each value on 1 to 448 neighbouring positions
- chain_embed: float32 [2, 128], replicated, may hold values from -4 to 4
- outgoing_ab: bfloat16 [128, 512], replicated, may hold values from -0.5 to 0.5
- outgoing_gate: bfloat16 [128, 128], replicated, may hold values from -0.5 to 0.5
- outgoing_final: bfloat16 [128, 128], replicated, may hold values from -0.5 to 0.5
- incoming_ab: bfloat16 [128, 512], replicated, may hold values from -0.5 to 0.5
- incoming_gate: bfloat16 [128, 128], replicated, may hold values from -0.5 to 0.5
- incoming_final: bfloat16 [128, 128], replicated, may hold values from -0.5 to 0.5
Outputs:
- pair_out: bfloat16 [896, 896, 128], P('row', 'col')
Inputs may be any that keep to these rules, and one draw needn't show every extreme that they name: `chain_index`: chain indices never fall along the residues; every chain has at least one residue and one chain has exactly 448.
All inputs are finite; a program needn't handle non-finite values.
Results may differ from a plain program's by a relative error of at most 0.0035.
Values may be sent and summed in bfloat16 or wider, within the bound.
A program may use at most 64 MiB of HBM per device.

v0:
```python
import jax
import jax.numpy as jnp
from jax import lax
from jax.sharding import PartitionSpec as P

EPSILON = 1e-05


def layer_norm(values, reduce_axes):
    center = values - jnp.mean(values, axis=reduce_axes, keepdims=True)
    spread = jnp.mean(center * center, axis=reduce_axes, keepdims=True)
    return center * lax.rsqrt(spread + EPSILON)


def triangle(pair_state, pair_mask, w_ab, w_gate, w_final, incoming):
    row_parts = lax.axis_size("row")
    col_parts = lax.axis_size("col")
    row_count, col_count, channels = pair_state.shape
    hidden = w_final.shape[0]
    normed = layer_norm(pair_state, (-1,)).astype(jnp.bfloat16)
    projected = jnp.einsum("ijc,ce->eij", normed, w_ab, preferred_element_type=jnp.float32)
    left_op = (
        jax.nn.sigmoid(projected[:hidden]) * projected[hidden : 2 * hidden] * pair_mask
    ).astype(jnp.bfloat16)
    right_op = (
        jax.nn.sigmoid(projected[2 * hidden : 3 * hidden]) * projected[3 * hidden :] * pair_mask
    ).astype(jnp.bfloat16)
    left_cut, right_cut = (
        lax.all_to_all(left_op, ("row", "col"), split_axis=0, concat_axis=1, tiled=True),
        lax.all_to_all(right_op, ("row", "col"), split_axis=0, concat_axis=1, tiled=True),
    )
    per_dev = left_cut.shape[0]

    def arrange(cut_piece):
        shaped = cut_piece.reshape(per_dev, row_parts, col_parts, row_count, col_count)
        return shaped.transpose(0, 1, 3, 2, 4).reshape(
            per_dev, row_parts * row_count, col_parts * col_count
        )

    left_plane = arrange(left_cut)
    right_plane = arrange(right_cut)
    gating = jax.nn.sigmoid(
        jnp.einsum("ijc,cd->ijd", normed, w_gate, preferred_element_type=jnp.float32)
    )
    if incoming:
        product = jnp.einsum(
            "cki,ckj->cij", left_plane, right_plane, preferred_element_type=jnp.float32
        )
    else:
        product = jnp.einsum(
            "cik,cjk->cij", left_plane, right_plane, preferred_element_type=jnp.float32
        )
    product = product.astype(jnp.bfloat16)
    per_dev = product.shape[0]
    pieces = product.reshape(per_dev, row_parts, row_count, col_parts, col_count)
    pieces = pieces.transpose(1, 3, 0, 2, 4).reshape(
        row_parts * col_parts * per_dev, row_count, col_count
    )
    returned = lax.all_to_all(pieces, ("row", "col"), split_axis=0, concat_axis=0, tiled=True)
    returned = returned.reshape(row_parts, col_parts, per_dev, row_count, col_count)
    einsum_form = "rsjab,rsjd->abd"
    product_float = returned.astype(jnp.float32)
    mixed_norm = layer_norm(product_float, (0, 1, 2)).astype(jnp.bfloat16)
    weights = w_final.reshape(row_parts, col_parts, per_dev, channels)
    update = jnp.einsum(einsum_form, mixed_norm, weights, preferred_element_type=jnp.float32)
    return pair_state + gating * update


def body(
    pair_repr,
    residue_mask,
    chain_index,
    chain_embed,
    outgoing_ab,
    outgoing_gate,
    outgoing_final,
    incoming_ab,
    incoming_gate,
    incoming_final,
):
    row_count, col_count, channels = pair_repr.shape
    row_start = lax.axis_index("row") * row_count
    col_start = lax.axis_index("col") * col_count
    mask_float = residue_mask.astype(jnp.float32)
    row_mask = lax.dynamic_slice_in_dim(mask_float, row_start, row_count)
    col_mask = lax.dynamic_slice_in_dim(mask_float, col_start, col_count)
    row_chain = lax.dynamic_slice_in_dim(chain_index, row_start, row_count)
    col_chain = lax.dynamic_slice_in_dim(chain_index, col_start, col_count)
    same_chain = row_chain[:, None] == col_chain[None, :]
    pair_state = pair_repr.astype(jnp.float32) + jnp.where(
        same_chain[:, :, None], chain_embed[1], chain_embed[0]
    )
    pair_mask = row_mask[:, None] * col_mask[None, :]
    pair_state = triangle(pair_state, pair_mask, outgoing_ab, outgoing_gate, outgoing_final, False)
    pair_state = triangle(pair_state, pair_mask, incoming_ab, incoming_gate, incoming_final, True)
    return pair_state.astype(jnp.bfloat16)


def solution(mesh):
    in_specs = (P("row", "col", None), P(), P(), P(), P(), P(), P(), P(), P(), P())
    out_specs = P("row", "col", None)
    return jax.shard_map(body, mesh=mesh, in_specs=in_specs, out_specs=out_specs, check_vma=False)
```

profile of v0, /device:TPU:1, one launch (start us, length us, event | category | flops | bytes accessed | tf_op | source)
XLA Modules:
  0.0 269.7 jit_solution(9412614245529814229)
XLA Ops:
  0.0 0.9 dynamic_slice.12
  0.9 0.8 dynamic_slice.13
  1.7 0.7 convert_element_type.73
  2.3 0.1 dynamic_slice.14
  2.4 0.1 dynamic_slice.15
  2.5 0.8 slice_bitcast_fusion.1
  3.2 0.1 broadcast_compare_fusion
  3.3 3.8 %fusion.29 = f32[56,112]{1,0:T(8,128)S(1)} fusion(bf16[56,112,128]{2,1,0:T(8,128)(2,1)} %param.10, f32[128]{0:T(128)S(1)} %get-tuple-element.10, f32[128]{0:T(128)S(1)} %get-tuple-element.9, pred[56,112]{1,0:T(8,128)(4,1)S(1)} %broadcast_compare_fusion), kind=kLoop, calls=%fused_computation.50 | loop fusion | flops 3204992 | bytes 1638016 | tf_op jit(solution)/shard_map/reduce_sum | solution.py:10
  7.2 5.7 %multiply_reduce_fusion.1 = f32[56,112]{1,0:T(8,128)S(1)} fusion(bf16[56,112,128]{2,1,0:T(8,128)(2,1)} %param.10, f32[56,112]{1,0:T(8,128)S(1)} %broadcast_multiply_fusion.4, f32[128]{0:T(128)S(1)} %get-tuple-element.10, f32[128]{0:T(128)S(1)} %get-tuple-element.9, pred[56,112]{1,0:T(8,128)(4,1)S(1)} %broadcast_compare_fusion), kind=kLoop, calls=%fused_computation.47 | loop fusion | flops 4810624 | bytes 1663104 | tf_op jit(solution)/shard_map/reduce_sum | solution.py:11
  12.9 2.7 %convolution_bitcast_fusion.1 = f32[512,56,112]{0,2,1:T(8,128)S(1)} fusion(bf16[56,112,128]{2,1,0:T(8,128)(2,1)S(1)} %copy-done.4, f32[56,112]{1,0:T(8,128)S(1)} %add_rsqrt_fusion.3, f32[56,112]{1,0:T(8,128)S(1)} %broadcast_multiply_fusion.4, f32[128]{0:T(128)S(1)} %get-tuple-element.10, f32[128]{0:T(128)S(1)} %get-tuple-element.9, ...), kind=kOutput, calls=%fused_computation.1 | convolution fusion | flops 826900480 | bytes 14639232 | tf_op jit(solution)/shard_map/ijc,ce->eij/dot_general | solution.py:21
  15.6 0.1 broadcast_multiply_fusion
  15.7 3.0 %fusion.19 = (bf16[128,56,112]{0,2,1:T(8,128)(2,1)}, bf16[128,56,112]{0,2,1:T(8,128)(2,1)S(1)}) fusion(f32[512,56,112]{0,2,1:T(8,128)S(1)} %convolution_bitcast_fusion.1, f32[56,112]{1,0:T(8,128)S(1)} %broadcast_multiply_fusion), kind=kLoop, calls=%fused_computation.30 | loop fusion | flops 9633792 | bytes 16081408 | tf_op jit(solution)/shard_map/convert_element_type | solution.py:27
  18.7 2.9 %copy.25 = bf16[128,56,112]{2,1,0:T(8,128)(2,1)} copy(bf16[128,56,112]{0,2,1:T(8,128)(2,1)S(1)} %get-tuple-element.8) | data formatting | bytes 3211264 | tf_op jit(solution)/shard_map/convert_element_type | solution.py:24
  21.6 12.0 %all-to-all-start = ((bf16[128,56,112]{2,1,0:T(8,128)(2,1)}), bf16[128,56,112]{2,1,0:T(8,128)(2,1)S(1)}, u32[]{:S(2)}, u32[]{:S(2)}) async-start(bf16[128,56,112]{2,1,0:T(8,128)(2,1)} %copy.25), calls=%async_computation | async-start | bytes 3670016 | tf_op jit(solution)/shard_map/all_to_all | solution.py:29
  33.6 3.8 %copy.27 = bf16[128,56,112]{2,1,0:T(8,128)(2,1)} copy(bf16[128,56,112]{0,2,1:T(8,128)(2,1)} %get-tuple-element.7) | data formatting | bytes 3211264 | tf_op jit(solution)/shard_map/convert_element_type | solution.py:27
  37.4 22.5 %all-to-all-done = bf16[128,56,112]{2,1,0:T(8,128)(2,1)S(1)} async-done(((bf16[128,56,112]{2,1,0:T(8,128)(2,1)}), bf16[128,56,112]{2,1,0:T(8,128)(2,1)S(1)}, u32[]{:S(2)}, u32[]{:S(2)}) %all-to-all-start) | async-done | bytes 1605664 | tf_op jit(solution)/shard_map/all_to_all | solution.py:29
  59.9 5.8 %all-to-all-start.1 = ((bf16[128,56,112]{2,1,0:T(8,128)(2,1)}), bf16[128,56,112]{2,1,0:T(8,128)(2,1)}, u32[]{:S(2)}, u32[]{:S(2)}) async-start(bf16[128,56,112]{2,1,0:T(8,128)(2,1)} %copy.27), calls=%async_computation.1 | async-start | bytes 3670016 | tf_op jit(solution)/shard_map/all_to_all | solution.py:30
  65.7 1.6 copy.26
  67.3 4.1 %reshape.209 = bf16[896,896]{1,0:T(8,128)(2,1)} reshape(bf16[1,16,56,8,112]{4,3,2,1,0:T(8,128)(2,1)} %copy.26) | data formatting | bytes 3211264 | tf_op jit(solution)/shard_map/reshape.6
  71.4 20.3 %all-to-all-done.1 = bf16[128,56,112]{2,1,0:T(8,128)(2,1)} async-done(((bf16[128,56,112]{2,1,0:T(8,128)(2,1)}), bf16[128,56,112]{2,1,0:T(8,128)(2,1)}, u32[]{:S(2)}, u32[]{:S(2)}) %all-to-all-start.1) | async-done | bytes 1605664 | tf_op jit(solution)/shard_map/all_to_all | solution.py:30
  91.7 1.9 copy.28
  93.5 2.4 reshape.211
  95.9 5.1 %convolution_convert_fusion.1 = bf16[896,896]{1,0:T(8,128)(2,1)} fusion(bf16[896,896]{1,0:T(8,128)(2,1)} %reshape.209, bf16[896,896]{1,0:T(8,128)(2,1)} %reshape.211), kind=kOutput, calls=%fused_computation.54 | convolution fusion | flops 1439449088 | bytes 4816896 | tf_op jit(solution)/shard_map/cik,cjk->cij/dot_general | solution.py:50
  101.0 3.7 %reshape.212 = bf16[1,16,56,8,112]{4,3,2,1,0:T(8,128)(2,1)S(1)} reshape(bf16[896,896]{1,0:T(8,128)(2,1)} %convolution_convert_fusion.1) | data formatting | bytes 3211264 | tf_op jit(solution)/shard_map/reshape | solution.py:55
  104.7 0.0 copy-start.9
  104.7 1.6 copy.29
  106.4 5.4 %all-to-all-start.2 = ((bf16[128,56,112]{2,1,0:T(8,128)(2,1)}), bf16[128,56,112]{2,1,0:T(8,128)(2,1)S(1)}, u32[]{:S(2)}, u32[]{:S(2)}) async-start(bf16[128,56,112]{2,1,0:T(8,128)(2,1)} %bitcast.60), calls=%async_computation.2 | async-start | bytes 3670016 | tf_op jit(solution)/shard_map/all_to_all | solution.py:59
  111.8 5.7 %fusion.32 = f32[56,112,128]{2,1,0:T(8,128)} fusion(bf16[56,112,128]{2,1,0:T(8,128)(2,1)} %param.10, f32[56,112]{1,0:T(8,128)S(1)} %add_rsqrt_fusion.3, f32[56,112]{1,0:T(8,128)S(1)} %broadcast_multiply_fusion.4, f32[128]{0:T(128)S(1)} %get-tuple-element.10, f32[128]{0:T(128)S(1)} %get-tuple-element.9, pred[56,112]{1,0:T(8,128)(4,1)S(1)} %broadcast_compare_fusion, ...), kind=kOutput, calls=%fused_computation.55 | convolution fusion | flops 210337792 | bytes 4907136 | tf_op jit(solution)/shard_map/ijc,cd->ijd/dot_general | solution.py:43
  117.5 20.6 %all-to-all-done.2 = bf16[128,56,112]{2,1,0:T(8,128)(2,1)S(1)} async-done(((bf16[128,56,112]{2,1,0:T(8,128)(2,1)}), bf16[128,56,112]{2,1,0:T(8,128)(2,1)S(1)}, u32[]{:S(2)}, u32[]{:S(2)}) %all-to-all-start.2) | async-done | bytes 1605664 | tf_op jit(solution)/shard_map/all_to_all | solution.py:59
  138.1 0.4 convert_reduce_fusion.1
  138.5 0.0 copy-start.10
  138.5 0.6 fusion.6
  139.2 0.5 fusion.7
  139.6 0.2 copy-done.5
  139.9 1.0 copy-done.12
  140.9 3.6 %fusion.40 = (f32[56,112]{1,0:T(8,128)S(1)}, f32[56,112,128]{2,1,0:T(8,128)S(1)}) fusion(bf16[128,128]{1,0:T(8,128)(2,1)S(1)} %copy-done.10, bf16[128,56,112]{2,1,0:T(8,128)(2,1)S(1)} %fusion.7, f32[56,112,128]{2,1,0:T(8,128)S(1)} %copy-done.12, f32[128]{0:T(128)S(1)} %get-tuple-element.10, f32[128]{0:T(128)S(1)} %get-tuple-element.9, ...), kind=kOutput, calls=%fused_computation.75 | convolution fusion | flops 212739968 | bytes 9698944 | tf_op jit(solution)/shard_map/rsjab,rsjd->abd/dot_general | solution.py:65
  144.5 0.0 copy-start.7
  144.5 2.1 multiply_reduce_fusion
  146.7 1.9 convolution_bitcast_fusion
  148.6 3.1 %fusion.9 = (bf16[128,56,112]{0,2,1:T(8,128)(2,1)}, bf16[128,56,112]{0,2,1:T(8,128)(2,1)S(1)}) fusion(f32[512,56,112]{0,2,1:T(8,128)S(1)} %convolution_bitcast_fusion, f32[56,112]{1,0:T(8,128)S(1)} %broadcast_multiply_fusion), kind=kLoop, calls=%fused_computation.16 | loop fusion | flops 9633792 | bytes 16081408 | tf_op jit(solution)/shard_map/convert_element_type | solution.py:27
  151.7 2.9 %copy.31 = bf16[128,56,112]{2,1,0:T(8,128)(2,1)} copy(bf16[128,56,112]{0,2,1:T(8,128)(2,1)S(1)} %get-tuple-element.6) | data formatting | bytes 3211264 | tf_op jit(solution)/shard_map/convert_element_type | solution.py:24
  154.5 5.4 %all-to-all-start.3 = ((bf16[128,56,112]{2,1,0:T(8,128)(2,1)}), bf16[128,56,112]{2,1,0:T(8,128)(2,1)S(1)}, u32[]{:S(2)}, u32[]{:S(2)}) async-start(bf16[128,56,112]{2,1,0:T(8,128)(2,1)} %copy.31), calls=%async_computation.3 | async-start | bytes 3670016 | tf_op jit(solution)/shard_map/all_to_all | solution.py:29
  159.9 3.8 %copy.33 = bf16[128,56,112]{2,1,0:T(8,128)(2,1)} copy(bf16[128,56,112]{0,2,1:T(8,128)(2,1)} %get-tuple-element.5) | data formatting | bytes 3211264 | tf_op jit(solution)/shard_map/convert_element_type | solution.py:27
  163.7 22.5 %all-to-all-done.3 = bf16[128,56,112]{2,1,0:T(8,128)(2,1)S(1)} async-done(((bf16[128,56,112]{2,1,0:T(8,128)(2,1)}), bf16[128,56,112]{2,1,0:T(8,128)(2,1)S(1)}, u32[]{:S(2)}, u32[]{:S(2)}) %all-to-all-start.3) | async-done | bytes 1605664 | tf_op jit(solution)/shard_map/all_to_all | solution.py:29
  186.2 5.8 %all-to-all-start.4 = ((bf16[128,56,112]{2,1,0:T(8,128)(2,1)}), bf16[128,56,112]{2,1,0:T(8,128)(2,1)}, u32[]{:S(2)}, u32[]{:S(2)}) async-start(bf16[128,56,112]{2,1,0:T(8,128)(2,1)} %copy.33), calls=%async_computation.4 | async-start | bytes 3670016 | tf_op jit(solution)/shard_map/all_to_all | solution.py:30
  192.0 1.7 copy.32
  193.7 4.1 %reshape.215 = bf16[896,896]{1,0:T(8,128)(2,1)} reshape(bf16[1,16,56,8,112]{4,3,2,1,0:T(8,128)(2,1)} %copy.32) | data formatting | bytes 3211264 | tf_op jit(solution)/shard_map/reshape.35
  197.8 20.2 %all-to-all-done.4 = bf16[128,56,112]{2,1,0:T(8,128)(2,1)} async-done(((bf16[128,56,112]{2,1,0:T(8,128)(2,1)}), bf16[128,56,112]{2,1,0:T(8,128)(2,1)}, u32[]{:S(2)}, u32[]{:S(2)}) %all-to-all-start.4) | async-done | bytes 1605664 | tf_op jit(solution)/shard_map/all_to_all | solution.py:30
  218.0 1.9 copy.34
  219.8 2.4 reshape.217
  222.2 5.1 %convolution_convert_fusion = bf16[896,896]{1,0:T(8,128)(2,1)} fusion(bf16[896,896]{1,0:T(8,128)(2,1)} %reshape.215, bf16[896,896]{1,0:T(8,128)(2,1)} %reshape.217), kind=kOutput, calls=%fused_computation.53 | convolution fusion | flops 1439449088 | bytes 4816896 | tf_op jit(solution)/shard_map/cki,ckj->cij/dot_general | solution.py:46
  227.4 3.7 %reshape.218 = bf16[1,16,56,8,112]{4,3,2,1,0:T(8,128)(2,1)S(1)} reshape(bf16[896,896]{1,0:T(8,128)(2,1)} %convolution_convert_fusion) | data formatting | bytes 3211264 | tf_op jit(solution)/shard_map/reshape | solution.py:55
  231.1 0.0 copy-start.8
  231.1 1.6 copy.35
  232.7 5.4 %all-to-all-start.5 = ((bf16[128,56,112]{2,1,0:T(8,128)(2,1)}), bf16[128,56,112]{2,1,0:T(8,128)(2,1)S(1)}, u32[]{:S(2)}, u32[]{:S(2)}) async-start(bf16[128,56,112]{2,1,0:T(8,128)(2,1)} %bitcast.61), calls=%async_computation.5 | async-start | bytes 3670016 | tf_op jit(solution)/shard_map/all_to_all | solution.py:59
  238.1 4.7 %fusion.33 = f32[56,112,128]{2,1,0:T(8,128)} fusion(f32[56,112,128]{2,1,0:T(8,128)} %copy-done.2, f32[56,112]{1,0:T(8,128)S(1)} %add_rsqrt_fusion.1, f32[56,112]{1,0:T(8,128)S(1)} %broadcast_multiply_fusion.2, bf16[128,128]{1,0:T(8,128)(2,1)S(1)} %copy-done.8), kind=kOutput, calls=%fused_computation.56 | convolution fusion | flops 207929344 | bytes 6505472 | tf_op jit(solution)/shard_map/ijc,cd->ijd/dot_general | solution.py:43
  242.8 21.6 %all-to-all-done.5 = bf16[128,56,112]{2,1,0:T(8,128)(2,1)S(1)} async-done(((bf16[128,56,112]{2,1,0:T(8,128)(2,1)}), bf16[128,56,112]{2,1,0:T(8,128)(2,1)S(1)}, u32[]{:S(2)}, u32[]{:S(2)}) %all-to-all-start.5) | async-done | bytes 1605664 | tf_op jit(solution)/shard_map/all_to_all | solution.py:59
  264.4 0.4 convert_reduce_fusion
  264.8 0.0 copy-start.11
  264.8 0.6 fusion.4
  265.5 0.5 fusion.5
  266.0 0.3 copy-done.6
  266.3 1.1 copy-done.3
  267.4 2.3 add_convert_fusion
  (25 shorter events, 0.1 us)
Async XLA Ops:
  0.0 12.9 %copy-start = (bf16[128,512]{1,0:T(8,128)(2,1)S(1)}, bf16[128,512]{1,0:T(8,128)(2,1)}, u32[]{:S(2)}) copy-start(bf16[128,512]{1,0:T(8,128)(2,1)} %param.14) | copy-start | bytes 393220
  0.0 12.9 %copy-start.4 = (bf16[56,112,128]{2,1,0:T(8,128)(2,1)S(1)}, bf16[56,112,128]{2,1,0:T(8,128)(2,1)}, u32[]{:S(2)}) copy-start(bf16[56,112,128]{2,1,0:T(8,128)(2,1)} %param.10) | copy-start | bytes 4816900
  21.6 38.3 %all-to-all-start = ((bf16[128,56,112]{2,1,0:T(8,128)(2,1)}), bf16[128,56,112]{2,1,0:T(8,128)(2,1)S(1)}, u32[]{:S(2)}, u32[]{:S(2)}) async-start(bf16[128,56,112]{2,1,0:T(8,128)(2,1)} %copy.25), calls=%async_computation | async-start | bytes 3670016 | tf_op jit(solution)/shard_map/all_to_all | solution.py:29
  59.9 31.8 %all-to-all-start.1 = ((bf16[128,56,112]{2,1,0:T(8,128)(2,1)}), bf16[128,56,112]{2,1,0:T(8,128)(2,1)}, u32[]{:S(2)}, u32[]{:S(2)}) async-start(bf16[128,56,112]{2,1,0:T(8,128)(2,1)} %copy.27), calls=%async_computation.1 | async-start | bytes 3670016 | tf_op jit(solution)/shard_map/all_to_all | solution.py:30
  104.7 7.1 %copy-start.9 = (bf16[128,128]{1,0:T(8,128)(2,1)S(1)}, bf16[128,128]{1,0:T(8,128)(2,1)}, u32[]{:S(2)}) copy-start(bf16[128,128]{1,0:T(8,128)(2,1)} %param.15) | copy-start | bytes 98308
  106.4 31.7 %all-to-all-start.2 = ((bf16[128,56,112]{2,1,0:T(8,128)(2,1)}), bf16[128,56,112]{2,1,0:T(8,128)(2,1)S(1)}, u32[]{:S(2)}, u32[]{:S(2)}) async-start(bf16[128,56,112]{2,1,0:T(8,128)(2,1)} %bitcast.60), calls=%async_computation.2 | async-start | bytes 3670016 | tf_op jit(solution)/shard_map/all_to_all | solution.py:59
  138.5 1.4 copy-start.5
  138.5 1.4 copy-start.10
  138.5 2.4 copy-start.12
  144.5 4.1 %copy-start.2 = (f32[56,112,128]{2,1,0:T(8,128)}, f32[56,112,128]{2,1,0:T(8,128)S(1)}, u32[]{:S(2)}) copy-start(f32[56,112,128]{2,1,0:T(8,128)S(1)} %get-tuple-element.12) | copy-start | bytes 9633796
  144.5 2.2 copy-start.7
  154.5 31.7 %all-to-all-start.3 = ((bf16[128,56,112]{2,1,0:T(8,128)(2,1)}), bf16[128,56,112]{2,1,0:T(8,128)(2,1)S(1)}, u32[]{:S(2)}, u32[]{:S(2)}) async-start(bf16[128,56,112]{2,1,0:T(8,128)(2,1)} %copy.31), calls=%async_computation.3 | async-start | bytes 3670016 | tf_op jit(solution)/shard_map/all_to_all | solution.py:29
  186.2 31.8 %all-to-all-start.4 = ((bf16[128,56,112]{2,1,0:T(8,128)(2,1)}), bf16[128,56,112]{2,1,0:T(8,128)(2,1)}, u32[]{:S(2)}, u32[]{:S(2)}) async-start(bf16[128,56,112]{2,1,0:T(8,128)(2,1)} %copy.33), calls=%async_computation.4 | async-start | bytes 3670016 | tf_op jit(solution)/shard_map/all_to_all | solution.py:30
  231.1 7.0 %copy-start.8 = (bf16[128,128]{1,0:T(8,128)(2,1)S(1)}, bf16[128,128]{1,0:T(8,128)(2,1)}, u32[]{:S(2)}) copy-start(bf16[128,128]{1,0:T(8,128)(2,1)} %param.18) | copy-start | bytes 98308
  232.7 31.7 %all-to-all-start.5 = ((bf16[128,56,112]{2,1,0:T(8,128)(2,1)}), bf16[128,56,112]{2,1,0:T(8,128)(2,1)S(1)}, u32[]{:S(2)}, u32[]{:S(2)}) async-start(bf16[128,56,112]{2,1,0:T(8,128)(2,1)} %bitcast.61), calls=%async_computation.5 | async-start | bytes 3670016 | tf_op jit(solution)/shard_map/all_to_all | solution.py:59
  264.4 1.9 copy-start.6
  264.8 2.6 copy-start.3
  264.8 2.6 copy-start.11
  267.4 2.3 copy-start.1
where the time goes:
time: 271 us; the launch traced here: 270 us
  waiting for transfers between devices  128 us (47%)
  local copies, waits for them, and re-layouts  49.2 us (18%)
  starting transfers between devices  39.8 us (15%)
  matrix products  31.1 us (11%)
  other arithmetic  21.7 us (8%)
    all_to_all x2, waiting for transfers between devices, triangle(): lax.all_to_all(left_op, ('row', 'col'), split_axis=0, concat_axis=1, tile...  45 us
    all_to_all x2, waiting for transfers between devices, triangle(): lax.all_to_all(pieces, ('row', 'col'), split_axis=0, concat_axis=0, tiled...  42.2 us
    all_to_all x2, waiting for transfers between devices, triangle(): lax.all_to_all(right_op, ('row', 'col'), split_axis=0, concat_axis=1, til...  40.5 us
    all_to_all x2, starting transfers between devices, triangle(): lax.all_to_all(left_op, ('row', 'col'), split_axis=0, concat_axis=1, tile...  17.4 us
    another operation x4, local copies, waits for them, and re-layouts  13 us
    all_to_all x2, starting transfers between devices, triangle(): lax.all_to_all(right_op, ('row', 'col'), split_axis=0, concat_axis=1, til...  11.6 us
    all_to_all x2, starting transfers between devices, triangle(): lax.all_to_all(pieces, ('row', 'col'), split_axis=0, concat_axis=0, tiled...  10.8 us
    reshape x4, local copies, waits for them, and re-layouts, triangle(): product.reshape(per_dev, row_parts, row_count, col_parts, col_count)  10.7 us
  transfers between devices with their start and end apart: 6, of which 6 were waited for; matrix products, arithmetic and copies ran while one was open for 11% of the time, Pallas kernels for 0%

commit v1 on v0

v1 whole, which is shorter than its diff:
```python
import jax
import jax.numpy as jnp
from jax import lax
from jax.experimental import pallas as pl
from jax.experimental.pallas import tpu as pltpu
from jax.sharding import PartitionSpec as P

EPSILON = 1e-05
MESH = pl.DeviceIdType.MESH
F32 = jnp.float32
BF16 = jnp.bfloat16

ROWS = 56
COLS = 112
LANES = 128
CH = 128
SKEW = 136


def peer(step, row, col):
    far = lax.rem(37 * step, 128)
    core = lax.rem(row + far, 2)
    x = lax.rem(row // 2 + far // 2, 4)
    z = lax.rem(col + far // 8, 4)
    y = lax.rem((col // 4) * 2 + row // 8 + far // 32, 4)
    return lax.rem(y, 2) * 8 + x * 2 + core, (y // 2) * 4 + z


def sigmoid(value):
    return 0.5 * jnp.tanh(0.5 * value) + 0.5


def kernel(
    x_ref, mask_ref, chain_ref, embed_ref,
    ab1_ref, gate1_ref, final1_ref, ab2_ref, gate2_ref, final2_ref,
    out_ref,
    state, normed, gating, stage, embed_t, ab_t, gate_t, final_t,
    left_out, right_out, prod_out, left_in, right_in, prod_in, left_panel, right_panel,
    send_sem, recv_sem, own_sem,
):
    row, col = lax.axis_index("row"), lax.axis_index("col")
    me = row * 8 + col
    barrier = pltpu.get_barrier_semaphore()

    def greet(step, carry):
        pl.semaphore_signal(barrier, inc=1, device_id=peer(step, row, col), device_id_type=MESH)
        return carry

    lax.fori_loop(1, 128, greet, 0)

    def turned(value):
        return value.astype(F32).T.astype(BF16)

    for update, (ab, gate, final) in enumerate(
        ((ab1_ref, gate1_ref, final1_ref), (ab2_ref, gate2_ref, final2_ref))
    ):
        for part in range(4):
            ab_t[update, part * CH : (part + 1) * CH, :] = turned(ab[:, part * CH : (part + 1) * CH])
        gate_t[update] = turned(gate[...])
        final_t[update] = turned(final[...])
    for kind in range(2):
        embed_t[kind] = jnp.broadcast_to(embed_ref[kind : kind + 1, :], (CH, CH)).T

    lane = lax.broadcasted_iota(jnp.int32, (1, LANES), 1)

    def collect(j, carry):
        mask, chain = carry
        here = lane == j
        mask = jnp.where(here, mask_ref[col * COLS + j].astype(F32), mask)
        return mask, jnp.where(here, chain_ref[col * COLS + j], chain)

    col_mask, col_chain = lax.fori_loop(
        0, COLS, collect, (jnp.zeros((1, LANES), F32), jnp.full((1, LANES), -1, jnp.int32))
    )

    def row_at(i):
        return pl.ds(pl.multiple_of(i * SKEW, 8), CH)

    def start_state(i):
        tile = jnp.concatenate([x_ref[i].astype(F32), jnp.zeros((LANES - COLS, CH), F32)], axis=0).T
        same = jnp.broadcast_to(col_chain == chain_ref[row * ROWS + i], (CH, LANES))
        return tile + jnp.where(same, embed_t[1], embed_t[0])

    def norm(value):
        center = value - jnp.sum(value, axis=0, keepdims=True) * (1.0 / CH)
        spread = jnp.sum(center * center, axis=0, keepdims=True) * (1.0 / CH)
        return (center * lax.rsqrt(spread + EPSILON)).astype(BF16)

    def operand(update, side, i, unit):
        weights = ab_t[update, side * 2 * CH : (side + 1) * 2 * CH, :]
        both = jnp.dot(weights, unit, preferred_element_type=F32)
        pair_mask = col_mask * mask_ref[row * ROWS + i].astype(F32)
        stage[row_at(i), :] = sigmoid(both[:CH]) * both[CH:] * pair_mask

    def exchange_start(source, target, where, number, row_to, col_to):
        pltpu.make_async_remote_copy(
            source, target.at[me], send_sem.at[number], recv_sem.at[number],
            device_id=(row_to, col_to), device_id_type=MESH,
        ).start()

    def relay(source, target, number):
        def gather(channel):
            source[channel] = stage[pl.ds(channel, ROWS, stride=SKEW), :].astype(BF16)

        def one(step, carry):
            row_to, col_to = peer(step, row, col)
            channel = row_to * 8 + col_to
            gather(channel)
            exchange_start(source.at[channel], target, None, number, row_to, col_to)
            return carry

        lax.fori_loop(1, 128, one, 0)
        gather(me)
        pltpu.make_async_copy(source.at[me], target.at[me], own_sem.at[number]).start()

    def arrive(source, target, number):
        pltpu.make_async_copy(source.at[me], target.at[me], own_sem.at[number]).wait()
        all_but_one = target.at[pl.ds(0, 127)]
        pltpu.make_async_copy(all_but_one, all_but_one, recv_sem.at[number]).wait()

    def sent(source, number):
        all_but_one = source.at[pl.ds(0, 127)]
        pltpu.make_async_copy(all_but_one, all_but_one, send_sem.at[number]).wait()

    for update in range(2):
        incoming = update == 1
        buffers = [b.at[update] for b in (left_out, right_out, prod_out, left_in, right_in, prod_in)]
        l_out, r_out, p_out, l_in, r_in, p_in = buffers
        base = update * 3

        def first(chunk, carry):
            for k in range(4):
                i = chunk * 4 + k
                if update == 0:
                    state[i] = start_state(i)
                else:
                    change = jnp.dot(final_t[0], stage[row_at(i), :].astype(BF16), preferred_element_type=F32)
                    state[i] = state[i] + gating[i] * change
                unit = norm(state[i])
                normed[i] = unit
                operand(update, 0, i, unit)
            return carry

        lax.fori_loop(0, ROWS // 4, first, 0)
        if update == 0:
            pl.semaphore_wait(barrier, 127)
        relay(l_out, l_in, base)

        def second(chunk, carry):
            for k in range(4):
                i = chunk * 4 + k
                operand(update, 1, i, normed[i])
            return carry

        lax.fori_loop(0, ROWS // 4, second, 0)
        relay(r_out, r_in, base + 1)

        def third(chunk, carry):
            for k in range(4):
                i = chunk * 4 + k
                gating[i] = sigmoid(jnp.dot(gate_t[update], normed[i], preferred_element_type=F32))
            return carry

        lax.fori_loop(0, ROWS // 4, third, 0)

        def panel(source, target, turn):
            def block(n, carry):
                high, low = n // 8, lax.rem(n, 8)
                tile = jnp.concatenate(
                    [
                        source[high * 16 + low].astype(F32),
                        source[high * 16 + 8 + low].astype(F32),
                        jnp.zeros((LANES - 2 * ROWS, LANES), F32),
                    ],
                    axis=0,
                )
                if turn:
                    high, low, tile = low, high, tile.T
                target[
                    pl.ds(pl.multiple_of(high * LANES, LANES), LANES),
                    pl.ds(pl.multiple_of(low * LANES, LANES), LANES),
                ] = tile.astype(BF16)
                return carry

            lax.fori_loop(0, 64, block, 0)

        arrive(l_out, l_in, base)
        panel(l_in, left_panel, incoming)
        arrive(r_out, r_in, base + 1)
        panel(r_in, right_panel, False)

        def multiply(n, carry):
            at = pl.ds(pl.multiple_of(n * 256, 256), 256)
            if incoming:
                part = jnp.dot(left_panel[...], right_panel[:, at], preferred_element_type=F32)
            else:
                part = lax.dot_general(
                    left_panel[...], right_panel[at, :], (((1,), (1,)), ((), ())), preferred_element_type=F32
                )
            for r in range(16):
                top = (r // 2) * LANES + (r % 2) * ROWS
                for s in range(2):
                    p_out[r * 8 + n * 2 + s] = part[top : top + ROWS, s * LANES : (s + 1) * LANES].astype(BF16)
            return carry

        lax.fori_loop(0, 4, multiply, 0)

        def give(step, carry):
            row_to, col_to = peer(step, row, col)
            exchange_start(p_out.at[row_to * 8 + col_to], p_in, None, base + 2, row_to, col_to)
            return carry

        lax.fori_loop(1, 128, give, 0)
        pltpu.make_async_copy(p_out.at[me], p_in.at[me], own_sem.at[base + 2]).start()
        arrive(p_out, p_in, base + 2)

        def add(c, total):
            return total + p_in[c].astype(F32)

        mean = lax.fori_loop(0, CH, add, jnp.zeros((ROWS, LANES), F32), unroll=8) * (1.0 / CH)

        def add_square(c, total):
            center = p_in[c].astype(F32) - mean
            return total + center * center

        spread = lax.fori_loop(0, CH, add_square, jnp.zeros((ROWS, LANES), F32), unroll=8) * (1.0 / CH)
        scale = lax.rsqrt(spread + EPSILON)

        def spread_out(c, carry):
            stage[pl.ds(c, ROWS, stride=SKEW), :] = (p_in[c].astype(F32) - mean) * scale
            return carry

        lax.fori_loop(0, CH, spread_out, 0, unroll=8)

    def last(chunk, carry):
        for k in range(4):
            i = chunk * 4 + k
            change = jnp.dot(final_t[1], stage[row_at(i), :].astype(BF16), preferred_element_type=F32)
            value = state[i] + gating[i] * change
            out_ref[i] = value.T[:COLS].astype(BF16)
        return carry

    lax.fori_loop(0, ROWS // 4, last, 0)
    for update in range(2):
        for number, source in enumerate((left_out, right_out, prod_out)):
            sent(source.at[update], update * 3 + number)


def body(*args):
    vmem, smem = (pl.BlockSpec(memory_space=m) for m in (pltpu.VMEM, pltpu.SMEM))
    tiles = pltpu.VMEM((2, CH, ROWS, LANES), BF16)
    return pl.pallas_call(
        kernel,
        out_shape=jax.ShapeDtypeStruct((ROWS, COLS, CH), BF16),
        in_specs=[vmem, smem, smem] + [vmem] * 7,
        out_specs=vmem,
        scratch_shapes=[
            pltpu.VMEM((ROWS, CH, LANES), F32),
            pltpu.VMEM((ROWS, CH, LANES), BF16),
            pltpu.VMEM((ROWS, CH, LANES), F32),
            pltpu.VMEM((ROWS * SKEW, LANES), F32),
            pltpu.VMEM((2, CH, LANES), F32),
            pltpu.VMEM((2, 4 * CH, CH), BF16),
            pltpu.VMEM((2, CH, CH), BF16),
            pltpu.VMEM((2, CH, CH), BF16),
            tiles, tiles, tiles, tiles, tiles, tiles,
            pltpu.VMEM((8 * LANES, 8 * LANES), BF16),
            pltpu.VMEM((8 * LANES, 8 * LANES), BF16),
            pltpu.SemaphoreType.DMA((6,)),
            pltpu.SemaphoreType.DMA((6,)),
            pltpu.SemaphoreType.DMA((6,)),
        ],
        compiler_params=pltpu.CompilerParams(
            collective_id=0, has_side_effects=True, vmem_limit_bytes=62 << 20
        ),
    )(*args)


def solution(mesh):
    in_specs = (P("row", "col", None), P(), P(), P(), P(), P(), P(), P(), P(), P())
    out_specs = P("row", "col", None)
    return jax.shard_map(body, mesh=mesh, in_specs=in_specs, out_specs=out_specs, check_vma=False)
```

time: 271 us -> 182 us (0.67)
  Pallas kernels: 0 us -> 179 us
  waiting for transfers between devices: 128 us -> 0 us
  local copies, waits for them, and re-layouts: 49.2 us -> 2.68 us
  starting transfers between devices: 39.8 us -> 0 us
  matrix products: 31.1 us -> 0 us
  other arithmetic: 21.7 us -> 0 us
    pallas_call x0 -> x1, Pallas kernels: none -> 179 us  [body(): pl.pallas_call(kernel, out_shape=jax.ShapeDtypeStruct((ROWS, COLS, CH), B...]
    all_to_all x6 -> x0, waiting for transfers between devices: 128 us -> none  [the longest x2 45 us: triangle(): lax.all_to_all(left_op, ('row', 'col'), split_axis=0, concat_axis=1, tile...]
    all_to_all x6 -> x0, starting transfers between devices: 39.8 us -> none  [the longest x2 17.4 us: triangle(): lax.all_to_all(left_op, ('row', 'col'), split_axis=0, concat_axis=1, tile...]
    dot_general x8 -> x0, matrix products: 31.1 us -> none  [the longest x2 10.3 us: triangle(): jnp.einsum('ijc,cd->ijd', normed, w_gate, preferred_element_type=jnp.floa...]
    reduce_sum x7 -> x0, other arithmetic: 13.7 us -> none  [the longest x4 9.09 us: layer_norm(): spread = jnp.mean(center * center, axis=reduce_axes, keepdims=True)]
    convert_element_type x4 -> x0, local copies, waits for them, and re-layouts: 13.3 us -> none  [the longest x2 7.58 us: triangle(): right_op = (jax.nn.sigmoid(projected[2 * hidden:3 * hidden]) * projected[...]
    another operation x4 -> x0, local copies, waits for them, and re-layouts: 13 us -> none
    reshape x4 -> x0, local copies, waits for them, and re-layouts: 10.7 us -> none  [triangle(): product.reshape(per_dev, row_parts, row_count, col_parts, col_count)]
  transfers between devices with their start and end apart: 6 -> 0, of which waited for: 6 -> 0; matrix products, arithmetic and copies ran while one was open for 11% -> 0% of each run, Pallas kernels for 0% -> 0%
where the time goes in v1:
time: 182 us
  Pallas kernels  179 us (98%)
  local copies, waits for them, and re-layouts  2.68 us (1%)
    pallas_call x1, Pallas kernels, body(): pl.pallas_call(kernel, out_shape=jax.ShapeDtypeStruct((ROWS, COLS, CH), B...  179 us

profile of v1, /device:TPU:1, one launch (start us, length us, event | category | flops | bytes accessed | tf_op | source)
XLA Modules:
  0.0 181.9 jit_solution(6549468883663480513)
XLA Ops:
  0.0 179.2 %shard_map.100 = bf16[56,112,128]{2,1,0:T(8,128)(2,1)} custom-call(bf16[56,112,128]{2,1,0:T(8,128)(2,1)} %x_ref.1, s32[896]{0:T(1024)} %mask_ref.1, s32[896]{0:T(1024)} %chain_ref.1, f32[2,128]{1,0:T(2,128)} %embed_ref.1, bf16[128,512]{1,0:T(8,128)(2,1)} %ab1_ref.1, bf16[128,128]{1,0:T(8,128)(2,1)} %gate1_ref.1, bf16[128,128]{1,0:T(8,128)(2,1)} %final1_ref.1, ...), custom_call_target="tpu_custom_call" | custom-call | tf_op jit(solution)/shard_map/pallas_call | solution.py:252
  179.2 2.7 %copy.12 = bf16[56,112,128]{2,1,0:T(8,128)(2,1)} copy(bf16[56,112,128]{2,1,0:T(8,128)(2,1)} %shard_map.100) | data formatting | bytes 3211264

commit v2 on v1

v2 whole, which is shorter than its diff:
```python
import jax
import jax.numpy as jnp
from jax import lax
from jax.experimental import pallas as pl
from jax.experimental.pallas import tpu as pltpu
from jax.sharding import PartitionSpec as P

EPSILON = 1e-05
MESH = pl.DeviceIdType.MESH
F32 = jnp.float32
BF16 = jnp.bfloat16

ROWS = 56
COLS = 112
LANES = 128
CH = 128
SKEW = 136
HALVES = ((0, 32), (32, 24))
WIDE = 256


def peer(step, row, col):
    far = lax.rem(37 * step, 128)
    core = lax.rem(row + far, 2)
    x = lax.rem(row // 2 + far // 2, 4)
    z = lax.rem(col + far // 8, 4)
    y = lax.rem((col // 4) * 2 + row // 8 + far // 32, 4)
    return lax.rem(y, 2) * 8 + x * 2 + core, (y // 2) * 4 + z


def sigmoid(value):
    return 0.5 * jnp.tanh(0.5 * value) + 0.5


def for_each_peer(one):
    def turn(n, carry):
        for k in range(4):
            one(1 + n * 4 + k)
        return carry

    lax.fori_loop(0, 31, turn, 0)
    for step in range(125, 128):
        one(step)


def kernel(
    x_ref, mask_ref, chain_ref, embed_ref,
    ab1_ref, gate1_ref, final1_ref, ab2_ref, gate2_ref, final2_ref,
    out_ref,
    state, normed, gating, stage, embed_t, ab_t, gate_t, final_t, left_panel, right_panel, total,
    out_a, out_b, in_a, in_b,
    send_sem, recv_sem,
):
    row, col = lax.axis_index("row"), lax.axis_index("col")
    me = row * 8 + col
    barrier = pltpu.get_barrier_semaphore()

    def greet(step):
        pl.semaphore_signal(barrier, inc=1, device_id=peer(step, row, col), device_id_type=MESH)

    for_each_peer(greet)

    def turned(value):
        return value.astype(F32).T.astype(BF16)

    for update, (ab, gate, final) in enumerate(
        ((ab1_ref, gate1_ref, final1_ref), (ab2_ref, gate2_ref, final2_ref))
    ):
        for part in range(4):
            ab_t[update, part * CH : (part + 1) * CH, :] = turned(ab[:, part * CH : (part + 1) * CH])
        gate_t[update] = turned(gate[...])
        final_t[update] = turned(final[...])
    for kind in range(2):
        embed_t[kind] = jnp.broadcast_to(embed_ref[kind : kind + 1, :], (CH, CH)).T

    lane = lax.broadcasted_iota(jnp.int32, (1, LANES), 1)

    def collect(j, carry):
        mask, chain = carry
        here = lane == j
        mask = jnp.where(here, mask_ref[col * COLS + j].astype(F32), mask)
        return mask, jnp.where(here, chain_ref[col * COLS + j], chain)

    col_mask, col_chain = lax.fori_loop(
        0, COLS, collect, (jnp.zeros((1, LANES), F32), jnp.full((1, LANES), -1, jnp.int32)), unroll=8
    )

    def row_at(i):
        return pl.ds(pl.multiple_of(i * SKEW, 8), CH)

    def start_state(i):
        tile = jnp.concatenate([x_ref[i].astype(F32), jnp.zeros((LANES - COLS, CH), F32)], axis=0).T
        same = jnp.broadcast_to(col_chain == chain_ref[row * ROWS + i], (CH, LANES))
        return tile + jnp.where(same, embed_t[1], embed_t[0])

    def norm(value):
        center = value - jnp.sum(value, axis=0, keepdims=True) * (1.0 / CH)
        spread = jnp.sum(center * center, axis=0, keepdims=True) * (1.0 / CH)
        return (center * lax.rsqrt(spread + EPSILON)).astype(BF16)

    def operand(update, side, rows, units):
        weights = ab_t[update, side * 2 * CH : (side + 1) * 2 * CH, :]
        both = jnp.dot(weights, jnp.concatenate(units, axis=1), preferred_element_type=F32)
        for k, i in enumerate(rows):
            pair_mask = col_mask * mask_ref[row * ROWS + i].astype(F32)
            one = both[:, k * LANES : (k + 1) * LANES]
            stage[row_at(i), :] = sigmoid(one[:CH]) * one[CH:] * pair_mask

    def for_rows(half, several, visit):
        begin, count = HALVES[half]

        def turn(n, carry):
            visit([begin + n * several + k for k in range(several)])
            return carry

        lax.fori_loop(0, count // several, turn, 0)

    LEFT, RIGHT, PRODUCT = 0, 1, 2
    outs, ins = (out_a, out_b), (in_a, in_b)

    def slot(update, kind, half):
        return (update * 3 + kind) * 2 + half

    def send(update, kind, half, row_to, col_to):
        number = slot(update, kind, half)
        pltpu.make_async_remote_copy(
            outs[half].at[update * 3 + kind, row_to * 8 + col_to], ins[half].at[update * 3 + kind, me],
            send_sem.at[number], recv_sem.at[number], device_id=(row_to, col_to), device_id_type=MESH,
        ).start()

    def relay(update, kind, half):
        begin, count = HALVES[half]

        def gather(channel):
            return stage[pl.ds(begin * SKEW + channel, count, stride=SKEW), :].astype(BF16)

        def one(step):
            row_to, col_to = peer(step, row, col)
            channel = row_to * 8 + col_to
            outs[half][update * 3 + kind, channel] = gather(channel)
            send(update, kind, half, row_to, col_to)

        for_each_peer(one)
        ins[half][update * 3 + kind, me] = gather(me)

    def arrive(update, kind, half):
        others = ins[half].at[update * 3 + kind, pl.ds(0, 127)]
        pltpu.make_async_copy(others, others, recv_sem.at[slot(update, kind, half)]).wait()

    def give(update, half):
        def one(step):
            row_to, col_to = peer(step, row, col)
            send(update, PRODUCT, half, row_to, col_to)

        for_each_peer(one)
        ins[half][update * 3 + PRODUCT, me] = outs[half][update * 3 + PRODUCT, me]

    def columns(visit):
        def turn(s, carry):
            visit(s, pl.ds(pl.multiple_of(s * LANES, LANES), LANES))
            return carry

        lax.fori_loop(0, 8, turn, 0)

    def received(update, kind, half, s):
        return [ins[half][update * 3 + kind, r * 8 + s].astype(F32) for r in range(16)]

    def plain_panel(update, kind, half, panel, first):
        count = HALVES[half][1]

        def visit(s, at):
            tiles = jnp.concatenate(received(update, kind, half, s), axis=0)
            panel[first : first + 16 * count, at] = tiles.astype(BF16)

        columns(visit)

    def turned_panel(update, kind, half, panel, first):
        count = HALVES[half][1]

        def visit(s, at):
            tiles = jnp.concatenate(received(update, kind, half, s), axis=0)
            panel[at, first : first + 16 * count] = tiles.T.astype(BF16)

        columns(visit)

    def padded_panel(update, kind, panel):
        def visit(s, at):
            one, two = received(update, kind, 0, s), received(update, kind, 1, s)
            nothing = jnp.zeros((LANES - 2 * ROWS, LANES), F32)
            for a in range(8):
                pieces = [one[2 * a], two[2 * a], one[2 * a + 1], two[2 * a + 1], nothing]
                panel[a * LANES : (a + 1) * LANES, at] = jnp.concatenate(pieces, axis=0).astype(BF16)

        columns(visit)

    def wide(visit):
        def turn(n, carry):
            visit(n, pl.ds(pl.multiple_of(n * WIDE, WIDE), WIDE))
            return carry

        lax.fori_loop(0, 8 * LANES // WIDE, turn, 0)

    def outgoing_product(half, first):
        count = HALVES[half][1]

        def visit(n, at):
            part = lax.dot_general(
                left_panel[first : first + 16 * count, :], right_panel[at, :], (((1,), (1,)), ((), ())),
                preferred_element_type=F32,
            )
            for r in range(16):
                for k in range(WIDE // LANES):
                    block = part[r * count : (r + 1) * count, k * LANES : (k + 1) * LANES]
                    outs[half][PRODUCT, r * 8 + n * (WIDE // LANES) + k] = block.astype(BF16)

        wide(visit)

    def incoming_first(depth):
        def visit(n, at):
            total[:, at] = jnp.dot(left_panel[:, :depth], right_panel[:depth, at], preferred_element_type=F32)

        wide(visit)

    def incoming_second(begin, end):
        def visit(n, at):
            part = total[:, at] + jnp.dot(
                left_panel[:, begin:end], right_panel[begin:end, at], preferred_element_type=F32
            )
            for r in range(16):
                for half, (top, count) in enumerate(HALVES):
                    top = (r // 2) * LANES + (r % 2) * ROWS + top
                    for k in range(WIDE // LANES):
                        block = part[top : top + count, k * LANES : (k + 1) * LANES]
                        outs[half][3 + PRODUCT, r * 8 + n * (WIDE // LANES) + k] = block.astype(BF16)

        wide(visit)

    def mix(update, half):
        begin, count = HALVES[half]
        which = update * 3 + PRODUCT
        nothing = jnp.zeros((count, LANES), F32)

        def add(c, carry):
            return carry + ins[half][which, c].astype(F32)

        mean = lax.fori_loop(0, CH, add, nothing, unroll=8) * (1.0 / CH)

        def add_square(c, carry):
            center = ins[half][which, c].astype(F32) - mean
            return carry + center * center

        spread = lax.fori_loop(0, CH, add_square, nothing, unroll=8) * (1.0 / CH)
        scale = lax.rsqrt(spread + EPSILON)

        def put(c, carry):
            center = ins[half][which, c].astype(F32) - mean
            stage[pl.ds(begin * SKEW + c, count, stride=SKEW), :] = center * scale
            return carry

        lax.fori_loop(0, CH, put, 0, unroll=8)

    def changed(update, rows):
        mixed = jnp.concatenate([stage[row_at(i), :].astype(BF16) for i in rows], axis=1)
        change = jnp.dot(final_t[update], mixed, preferred_element_type=F32)
        return [
            state[i] + gating[i] * change[:, k * LANES : (k + 1) * LANES] for k, i in enumerate(rows)
        ]

    def first(update):
        def visit(rows):
            values = [start_state(i) for i in rows] if update == 0 else changed(0, rows)
            units = [norm(value) for value in values]
            for i, value, unit in zip(rows, values, units):
                state[i] = value
                normed[i] = unit
            operand(update, RIGHT, rows, units)

        return visit

    def second(update):
        def visit(rows):
            operand(update, LEFT, rows, [normed[i] for i in rows])

        return visit

    def third(update):
        def visit(rows):
            units = jnp.concatenate([normed[i] for i in rows], axis=1)
            gates = sigmoid(jnp.dot(gate_t[update], units, preferred_element_type=F32))
            for k, i in enumerate(rows):
                gating[i] = gates[:, k * LANES : (k + 1) * LANES]

        return visit

    def last(rows):
        for i, value in zip(rows, changed(1, rows)):
            out_ref[i] = value.T[:COLS].astype(BF16)

    for_rows(0, 4, first(0))
    pl.semaphore_wait(barrier, 127)
    relay(0, RIGHT, 0)
    for_rows(1, 4, first(0))
    relay(0, RIGHT, 1)
    for half in range(2):
        for_rows(half, 4, second(0))
        relay(0, LEFT, half)
    for half in range(2):
        for_rows(half, 4, third(0))
    arrive(0, RIGHT, 0)
    arrive(0, RIGHT, 1)
    padded_panel(0, RIGHT, right_panel)
    for half, place in ((0, 0), (1, 512)):
        arrive(0, LEFT, half)
        plain_panel(0, LEFT, half, left_panel, place)
        outgoing_product(half, place)
        give(0, half)

    for half in range(2):
        arrive(0, PRODUCT, half)
        mix(0, half)
        for_rows(half, 4, first(1))
        relay(1, RIGHT, half)
        for_rows(half, 4, second(1))
        relay(1, LEFT, half)
    for half in range(2):
        for_rows(half, 4, third(1))
    for half, place in ((0, 0), (1, 512)):
        arrive(1, RIGHT, half)
        plain_panel(1, RIGHT, half, right_panel, place)
        arrive(1, LEFT, half)
        turned_panel(1, LEFT, half, left_panel, place)
        if half == 0:
            incoming_first(512)
        else:
            incoming_second(512, 896)
    for half in range(2):
        give(1, half)
    for half in range(2):
        arrive(1, PRODUCT, half)
        mix(1, half)
        for_rows(half, 4, last)

    for update in range(2):
        for kind in range(3):
            for half in range(2):
                others = outs[half].at[update * 3 + kind, pl.ds(0, 127)]
                pltpu.make_async_copy(others, others, send_sem.at[slot(update, kind, half)]).wait()


def body(*args):
    vmem, smem = (pl.BlockSpec(memory_space=m) for m in (pltpu.VMEM, pltpu.SMEM))
    tiles_a = pltpu.VMEM((6, CH, HALVES[0][1], LANES), BF16)
    tiles_b = pltpu.VMEM((6, CH, HALVES[1][1], LANES), BF16)
    return pl.pallas_call(
        kernel,
        out_shape=jax.ShapeDtypeStruct((ROWS, COLS, CH), BF16),
        in_specs=[vmem, smem, smem] + [vmem] * 7,
        out_specs=vmem,
        scratch_shapes=[
            pltpu.VMEM((ROWS, CH, LANES), F32),
            pltpu.VMEM((ROWS, CH, LANES), BF16),
            pltpu.VMEM((ROWS, CH, LANES), F32),
            pltpu.VMEM((ROWS * SKEW, LANES), F32),
            pltpu.VMEM((2, CH, LANES), F32),
            pltpu.VMEM((2, 4 * CH, CH), BF16),
            pltpu.VMEM((2, CH, CH), BF16),
            pltpu.VMEM((2, CH, CH), BF16),
            pltpu.VMEM((8 * LANES, 8 * LANES), BF16),
            pltpu.VMEM((8 * LANES, 8 * LANES), BF16),
            pltpu.VMEM((8 * LANES, 8 * LANES), F32),
            tiles_a, tiles_b, tiles_a, tiles_b,
            pltpu.SemaphoreType.DMA((12,)),
            pltpu.SemaphoreType.DMA((12,)),
        ],
        compiler_params=pltpu.CompilerParams(
            collective_id=0, has_side_effects=True, vmem_limit_bytes=62 << 20
        ),
    )(*args)


def solution(mesh):
    in_specs = (P("row", "col", None), P(), P(), P(), P(), P(), P(), P(), P(), P())
    out_specs = P("row", "col", None)
    return jax.shard_map(body, mesh=mesh, in_specs=in_specs, out_specs=out_specs, check_vma=False)
```

time: 182 us -> 155 us (0.85)
  Pallas kernels: 179 us -> 152 us
    pallas_call x1, Pallas kernels: 179 us -> 152 us  [body(): pl.pallas_call(kernel, out_shape=jax.ShapeDtypeStruct((ROWS, COLS, CH), B...]
where the time goes in v2:
time: 155 us; the launch traced here: 154 us
  Pallas kernels  152 us (98%)
  local copies, waits for them, and re-layouts  2.68 us (2%)
    pallas_call x1, Pallas kernels, body(): pl.pallas_call(kernel, out_shape=jax.ShapeDtypeStruct((ROWS, COLS, CH), B...  152 us

profile of v2, /device:TPU:1, one launch (start us, length us, event | category | flops | bytes accessed | tf_op | source)
XLA Modules:
  0.0 154.5 jit_solution(5254128949619199581)
XLA Ops:
  0.0 151.8 %shard_map.100 = bf16[56,112,128]{2,1,0:T(8,128)(2,1)} custom-call(bf16[56,112,128]{2,1,0:T(8,128)(2,1)} %x_ref.1, s32[896]{0:T(1024)} %mask_ref.1, s32[896]{0:T(1024)} %chain_ref.1, f32[2,128]{1,0:T(2,128)} %embed_ref.1, bf16[128,512]{1,0:T(8,128)(2,1)} %ab1_ref.1, bf16[128,128]{1,0:T(8,128)(2,1)} %gate1_ref.1, bf16[128,128]{1,0:T(8,128)(2,1)} %final1_ref.1, ...), custom_call_target="tpu_custom_call" | custom-call | tf_op jit(solution)/shard_map/pallas_call | solution.py:354
  151.8 2.7 %copy.12 = bf16[56,112,128]{2,1,0:T(8,128)(2,1)} copy(bf16[56,112,128]{2,1,0:T(8,128)(2,1)} %shard_map.100) | data formatting | bytes 3211264

commit v3 on v0

v3 whole, which is shorter than its diff:
```python
import jax
import jax.numpy as jnp
from jax import lax
from jax.experimental import pallas as pl
from jax.experimental.pallas import tpu as pltpu
from jax.sharding import PartitionSpec as P

EPSILON = 1e-05
MESH = pl.DeviceIdType.MESH
F32 = jnp.float32
BF16 = jnp.bfloat16

ROWS = 56
COLS = 112
LANES = 128
TILES = 49
CH = 128
GROUP = 8
SHIFT = LANES - COLS
SKEW = 136
WIDE = 256
FIRST = 24
RA, RB, LA, LB, LX, PA, PB, PX = range(8)
MESSAGES = (24, 24, 32, 16, 2, 24, 24, 2) + (24, 24, 24, 24, 2, 24, 24, 2)


def peer(step, row, col):
    far = lax.rem(37 * step, 128)
    core = lax.rem(row + far, 2)
    x = lax.rem(row // 2 + far // 2, 4)
    z = lax.rem(col + far // 8, 4)
    y = lax.rem((col // 4) * 2 + row // 8 + far // 32, 4)
    return lax.rem(y, 2) * 8 + x * 2 + core, (y // 2) * 4 + z


def sigmoid(value):
    return 0.5 * jnp.tanh(0.5 * value) + 0.5


def for_each_peer(one):
    def turn(n, carry):
        for k in range(4):
            one(1 + n * 4 + k)
        return carry

    lax.fori_loop(0, 31, turn, 0)
    for step in range(125, 128):
        one(step)


def kernel(
    x_hbm, mask_ref, chain_ref, embed_ref,
    ab1_ref, gate1_ref, final1_ref, ab2_ref, gate2_ref, final2_ref,
    out_ref,
    x_ref, state, normed, gating, stage, pair_mask, same_chain, embed_t, ab_t, gate_t, final_t,
    left_panel, right_panel, total, spare, kept, products, flat, flat_product,
    *rest,
):
    outs, ins = rest[:16], rest[16:32]
    send_sem, recv_sem, x_sem = rest[32:]
    row, col = lax.axis_index("row"), lax.axis_index("col")
    me = row * 8 + col
    barrier = pltpu.get_barrier_semaphore()

    def greet(row_to, col_to):
        pl.semaphore_signal(barrier, inc=1, device_id=(row_to, col_to), device_id_type=MESH)

    def greet_row(n, carry):
        for k in range(8):
            greet(lax.rem(row + n, 16), k)
        return carry

    for k in range(1, 8):
        greet(row, lax.rem(col + k, 8))
    lax.fori_loop(1, 16, greet_row, 0)
    x_copies = []
    for number, (begin, end) in enumerate(((0, FIRST * LANES), (FIRST * LANES, TILES * LANES))):
        at = pl.ds(begin, end - begin)
        x_copies.append(pltpu.make_async_copy(x_hbm.at[at], x_ref.at[at], x_sem.at[number]))
        x_copies[number].start()

    def turned(value):
        return value.astype(F32).T.astype(BF16)

    def turn_ab(update, ab, side):
        for part in (2 * side, 2 * side + 1):
            ab_t[update, part * CH : (part + 1) * CH, :] = turned(ab[:, part * CH : (part + 1) * CH])

    lane = lax.broadcasted_iota(jnp.int32, (1, LANES), 1)

    def collect(j, carry):
        mask, chain = carry
        here = lane == j
        mask = jnp.where(here, mask_ref[col * COLS + j], mask)
        return mask, jnp.where(here, chain_ref[col * COLS + j], chain)

    nothing = jnp.zeros((1, LANES), jnp.int32)
    col_mask, col_chain = lax.fori_loop(0, COLS, collect, (nothing, nothing), unroll=8)
    for phase in range(7):
        skip = SHIFT * phase

        def wrapped(value):
            value = value.astype(F32)
            near = pltpu.roll(value, LANES - skip, 1) if skip else value
            return jnp.where(lane < COLS - skip, near, pltpu.roll(value, COLS - skip, 1))

        tile_mask, tile_chain = wrapped(col_mask), wrapped(col_chain)
        for t in range(phase, TILES, 7):
            i = row * ROWS + t + t // 7
            near = lane < COLS - skip
            own_mask = jnp.where(near, mask_ref[i].astype(F32), mask_ref[i + 1].astype(F32))
            own_chain = jnp.where(near, chain_ref[i].astype(F32), chain_ref[i + 1].astype(F32))
            pair_mask[t : t + 1, :] = tile_mask * own_mask
            same_chain[t : t + 1, :] = jnp.where(tile_chain == own_chain, 1.0, 0.0)
    flat[...] = jnp.zeros(flat.shape, F32)

    lanes = lax.broadcasted_iota(jnp.int32, (GROUP, LANES), 1)
    row_of = lax.broadcasted_iota(jnp.int32, (GROUP, LANES), 0)
    from_former = lanes >= LANES - SHIFT * row_of
    from_same = lanes < COLS - SHIFT * row_of
    turn_back = (lanes + SHIFT * row_of) % LANES

    def unfold(tiles):
        mixed = jnp.where(from_former, pltpu.roll(tiles, 1, 0), tiles)
        return pltpu.roll(mixed, 0, 1, stride=SHIFT, stride_axis=0)

    def fold(rows):
        moved = jnp.take_along_axis(rows, turn_back, axis=1, mode="promise_in_bounds")
        return jnp.where(from_same, moved, pltpu.roll(moved, GROUP - 1, 0))

    def tile_at(t):
        return pl.ds(pl.multiple_of(t * SKEW, 8), CH)

    def positions(t):
        return pl.ds(pl.multiple_of(t * LANES, LANES), LANES)

    def start_state(t):
        same = jnp.broadcast_to(same_chain[pl.ds(t, 1), :], (CH, LANES)) > 0.5
        return x_ref[positions(t), :].astype(F32).T + jnp.where(same, embed_t[1], embed_t[0])

    def norm(value):
        center = value - jnp.sum(value, axis=0, keepdims=True) * (1.0 / CH)
        spread = jnp.sum(center * center, axis=0, keepdims=True) * (1.0 / CH)
        return (center * lax.rsqrt(spread + EPSILON)).astype(BF16)

    def operand(update, side, tiles, units):
        weights = ab_t[update, side * 2 * CH : (side + 1) * 2 * CH, :]
        both = jnp.dot(weights, jnp.concatenate(units, axis=1), preferred_element_type=F32)
        for k, t in enumerate(tiles):
            one = both[:, k * LANES : (k + 1) * LANES]
            stage[tile_at(t), :] = sigmoid(one[:CH]) * one[CH:] * pair_mask[pl.ds(t, 1), :]

    def for_tiles(begin, end, visit):
        def turn(n, carry):
            visit([begin + n * 4 + k for k in range(4)])
            return carry

        turns = (end - begin) // 4
        lax.fori_loop(0, turns, turn, 0)
        if begin + turns * 4 < end:
            visit(list(range(begin + turns * 4, end)))

    LEFT, RIGHT = 0, 1

    def send(number, row_to, col_to):
        pltpu.make_async_remote_copy(
            outs[number].at[row_to * 8 + col_to], ins[number].at[me],
            send_sem.at[number], recv_sem.at[number], device_id=(row_to, col_to), device_id_type=MESH,
        ).start()

    def staged(channel, begin, count):
        return stage[pl.ds(begin * SKEW + channel, count, stride=SKEW), :]

    def relay(make):
        def one(step):
            row_to, col_to = peer(step, row, col)
            channel = row_to * 8 + col_to
            for number, value in make(channel):
                outs[number][channel] = value.astype(BF16)
                send(number, row_to, col_to)

        for_each_peer(one)
        for number, value in make(me):
            ins[number][me] = value.astype(BF16)

    def arrive(*numbers):
        for number in numbers:
            others = ins[number].at[pl.ds(0, 127)]
            pltpu.make_async_copy(others, others, recv_sem.at[number]).wait()

    def give(*numbers):
        def one(step):
            row_to, col_to = peer(step, row, col)
            for number in numbers:
                send(number, row_to, col_to)

        for_each_peer(one)
        for number in numbers:
            ins[number][me] = outs[number][me]

    def got(number, source):
        return ins[number][source].astype(F32)

    def columns(visit):
        def turn(s, carry):
            visit(s, pl.ds(pl.multiple_of(s * LANES, LANES), LANES))
            return carry

        lax.fori_loop(0, 8, turn, 0)

    def wide(visit):
        def turn(n, carry):
            visit(n, pl.ds(pl.multiple_of(n * WIDE, WIDE), WIDE))
            return carry

        lax.fori_loop(0, 8 * LANES // WIDE, turn, 0)

    def unfolded(r, begin, end):
        return [unfold(flat[r, 7 * g : 7 * g + GROUP]) for g in range(begin, end)]

    def folded(slot, begin, rows):
        for g in range(rows.shape[0] // GROUP):
            at = 7 * (begin + g)
            flat_product[slot, at : at + GROUP] = fold(rows[g * GROUP : (g + 1) * GROUP])

    def mix(update, half):
        begin, count, padded = ((0, FIRST, FIRST), (FIRST, TILES - FIRST, 32))[half]
        pa, pb, px = (update * 8 + number for number in (PA, PB, PX))

        def add(c, carry):
            if half == 0:
                tile = got(pa, c)
            else:
                tile = jnp.concatenate([got(pb, c), jnp.broadcast_to(got(px, c)[0:1], (GROUP, LANES))], axis=0)
            products[c, :padded] = tile
            return carry + tile

        empty = jnp.zeros((padded, LANES), F32)
        mean = lax.fori_loop(0, CH, add, empty, unroll=8) * (1.0 / CH)

        def add_square(c, carry):
            center = products[c, :padded] - mean
            return carry + center * center

        spread = lax.fori_loop(0, CH, add_square, empty, unroll=8) * (1.0 / CH)
        scale = lax.rsqrt(spread + EPSILON)

        def put(c, carry):
            value = (products[c, :padded] - mean) * scale
            stage[pl.ds(begin * SKEW + c, count, stride=SKEW), :] = value[:count]
            return carry

        lax.fori_loop(0, CH, put, 0, unroll=8)

    def changed(update, tiles):
        mixed = jnp.concatenate([stage[tile_at(t), :].astype(BF16) for t in tiles], axis=1)
        change = jnp.dot(final_t[update], mixed, preferred_element_type=F32)
        return [
            state[t] + gating[t] * change[:, k * LANES : (k + 1) * LANES] for k, t in enumerate(tiles)
        ]

    def first(update):
        def visit(tiles):
            values = [start_state(t) for t in tiles] if update == 0 else changed(0, tiles)
            units = [norm(value) for value in values]
            for t, value, unit in zip(tiles, values, units):
                state[t] = value
                normed[t] = unit
            operand(update, RIGHT, tiles, units)

        return visit

    def second(update):
        def visit(tiles):
            operand(update, LEFT, tiles, [normed[t] for t in tiles])

        return visit

    def third(update):
        def visit(tiles):
            units = jnp.concatenate([normed[t] for t in tiles], axis=1)
            gates = sigmoid(jnp.dot(gate_t[update], units, preferred_element_type=F32))
            for k, t in enumerate(tiles):
                gating[t] = gates[:, k * LANES : (k + 1) * LANES]

        return visit

    def last(tiles):
        for t, value in zip(tiles, changed(1, tiles)):
            out_ref[positions(t), :] = value.T.astype(BF16)

    turn_ab(0, ab1_ref, RIGHT)
    for kind in range(2):
        embed_t[kind] = jnp.broadcast_to(embed_ref[kind : kind + 1, :], (CH, CH)).T
    x_copies[0].wait()
    for_tiles(0, FIRST, first(0))

    def right_first(channel):
        return [(RA, staged(channel, 0, FIRST))]

    def right_second(channel):
        spare[channel] = staged(channel, TILES - 1, 1)
        return [(RB, staged(channel, FIRST, 24))]

    def left_first(channel):
        tile = staged(channel, 0, 32)
        end = jnp.where(row_of == 7, jnp.broadcast_to(spare[channel], (GROUP, LANES)), tile[24:])
        return [(LA, jnp.concatenate([tile[:24], end], axis=0))]

    def left_second(channel):
        return [(LB, staged(channel, 31, 16)), (LX, staged(channel, 47, 2))]

    pl.semaphore_wait(barrier, 127)
    relay(right_first)
    x_copies[1].wait()
    for_tiles(FIRST, TILES, first(0))
    relay(right_second)
    turn_ab(0, ab1_ref, LEFT)
    for_tiles(0, TILES, second(0))
    relay(left_first)
    relay(left_second)
    for update, (gate, final) in enumerate(((gate1_ref, final1_ref), (gate2_ref, final2_ref))):
        gate_t[update] = turned(gate[...])
        final_t[update] = turned(final[...])
    for side in (LEFT, RIGHT):
        turn_ab(1, ab2_ref, side)
    for_tiles(0, TILES, third(0))

    def right_columns(s, at):
        empty = jnp.zeros((LANES - 2 * ROWS, LANES), F32)
        for r in range(16):
            source = r * 8 + s
            flat[r, 0:24] = got(RA, source)
            flat[r, 24:48] = got(RB, source)
            flat[r, 48:49] = got(LA, source)[31:32]
        for a in range(8):
            rows = unfolded(2 * a, 0, 7) + unfolded(2 * a + 1, 0, 7)
            rows = [jnp.where(lanes < COLS, part, 0.0) for part in rows]
            right_panel[a * LANES : (a + 1) * LANES, at] = jnp.concatenate(rows + [empty], axis=0).astype(BF16)

    def left_columns_first(s, at):
        rows = []
        for r in range(16):
            flat[r, 0:32] = got(LA, r * 8 + s)
            rows += unfolded(r, 0, 4)
        left_panel[:512, at] = jnp.concatenate(rows, axis=0).astype(BF16)

    def left_columns_second(s, at):
        rows = []
        for r in range(16):
            source = r * 8 + s
            flat[r, 24:32] = got(LA, source)[24:32]
            flat[r, 31:47] = got(LB, source)
            flat[r, 47:49] = got(LX, source)
            rows += unfolded(r, 4, 7)
        left_panel[512:896, at] = jnp.concatenate(rows, axis=0).astype(BF16)

    def outgoing_product(begin, end, half):
        count = (end - begin) // 16

        def visit(n, at):
            part = lax.dot_general(
                left_panel[begin:end, :], right_panel[at, :], (((1,), (1,)), ((), ())),
                preferred_element_type=F32,
            )
            for r in range(16):
                for k in range(WIDE // LANES):
                    block = part[r * count : (r + 1) * count, k * LANES : (k + 1) * LANES]
                    dest = r * 8 + n * (WIDE // LANES) + k
                    slot = r * 2 + k
                    if half == 0:
                        folded(slot, 0, block)
                        outs[PA][dest] = flat_product[slot, 0:24].astype(BF16)
                        kept[dest] = flat_product[slot, 24:32]
                    else:
                        flat_product[slot, 24:32] = kept[dest]
                        folded(slot, 4, block)
                        outs[PB][dest] = flat_product[slot, 24:48].astype(BF16)
                        outs[PX][dest] = flat_product[slot, 48:50].astype(BF16)

        wide(visit)

    arrive(RA, RB, LA)
    columns(right_columns)
    columns(left_columns_first)
    outgoing_product(0, 512, 0)
    give(PA)
    arrive(LB, LX)
    columns(left_columns_second)
    outgoing_product(512, 896, 1)
    give(PB, PX)

    def right_one(channel):
        return [(8 + RA, staged(channel, 0, FIRST))]

    def left_one(channel):
        return [(8 + LA, staged(channel, 0, FIRST))]

    def right_two(channel):
        spare[channel] = staged(channel, TILES - 1, 1)
        return [(8 + RB, staged(channel, FIRST, 24))]

    def left_two(channel):
        extra = jnp.concatenate([spare[channel], staged(channel, TILES - 1, 1)], axis=0)
        return [(8 + LB, staged(channel, FIRST, 24)), (8 + LX, extra)]

    arrive(PA)
    mix(0, 0)
    for_tiles(0, FIRST, first(1))
    relay(right_one)
    for_tiles(0, FIRST, second(1))
    relay(left_one)
    arrive(PB, PX)
    mix(0, 1)
    for_tiles(FIRST, TILES, first(1))
    relay(right_two)
    for_tiles(FIRST, TILES, second(1))
    relay(left_two)
    for_tiles(0, TILES, third(1))

    def incoming_columns(begin, end, numbers, turn):
        first_group, last_group = begin // GROUP, end // GROUP
        depth = pl.ds(16 * begin, 16 * (end - begin))

        def visit(s, at):
            rows = []
            for r in range(16):
                source = r * 8 + s
                flat[r, 0:24] = got(numbers[0], source)
                if end == ROWS:
                    flat[r, 24:48] = got(numbers[1], source)
                    extra = got(8 + LX, source)
                    flat[r, 48:49] = extra[1:2] if turn else extra[0:1]
                rows += unfolded(r, first_group, last_group)
            rows = jnp.concatenate(rows, axis=0)
            if turn:
                left_panel[at, depth] = rows.T.astype(BF16)
            else:
                right_panel[depth, at] = rows.astype(BF16)

        columns(visit)

    def incoming_first(n, at):
        total[:, at] = jnp.dot(left_panel[:, :384], right_panel[:384, at], preferred_element_type=F32)

    def incoming_second(n, at):
        part = total[:, at] + jnp.dot(
            left_panel[:, 384:896], right_panel[384:896, at], preferred_element_type=F32
        )
        for r in range(16):
            top = (r // 2) * LANES + (r % 2) * ROWS
            for k in range(WIDE // LANES):
                dest = r * 8 + n * (WIDE // LANES) + k
                slot = r * 2 + k
                folded(slot, 0, part[top : top + ROWS, k * LANES : (k + 1) * LANES])
                outs[8 + PA][dest] = flat_product[slot, 0:24].astype(BF16)
                outs[8 + PB][dest] = flat_product[slot, 24:48].astype(BF16)
                outs[8 + PX][dest] = flat_product[slot, 48:50].astype(BF16)

    rights, lefts = (8 + RA, 8 + RB), (8 + LA, 8 + LB)
    arrive(8 + RA)
    incoming_columns(0, 24, rights, False)
    arrive(8 + LA)
    incoming_columns(0, 24, lefts, True)
    wide(incoming_first)
    arrive(8 + RB, 8 + LB, 8 + LX)
    incoming_columns(24, 56, rights, False)
    incoming_columns(24, 56, lefts, True)
    wide(incoming_second)
    give(8 + PA)
    give(8 + PB, 8 + PX)
    arrive(8 + PA)
    mix(1, 0)
    for_tiles(0, FIRST, last)
    arrive(8 + PB, 8 + PX)
    mix(1, 1)
    for_tiles(FIRST, TILES, last)

    for number in range(16):
        others = outs[number].at[pl.ds(0, 127)]
        pltpu.make_async_copy(others, others, send_sem.at[number]).wait()


def body(pair_repr, *args):
    vmem, smem = (pl.BlockSpec(memory_space=m) for m in (pltpu.VMEM, pltpu.SMEM))
    messages = [pltpu.VMEM((CH, count, LANES), BF16) for count in MESSAGES]
    flat_shape = (TILES * LANES, CH)
    out = pl.pallas_call(
        kernel,
        out_shape=jax.ShapeDtypeStruct(flat_shape, BF16),
        in_specs=[pl.BlockSpec(memory_space=pl.ANY), smem, smem] + [vmem] * 7,
        out_specs=vmem,
        scratch_shapes=[
            pltpu.VMEM(flat_shape, BF16),
            pltpu.VMEM((TILES, CH, LANES), F32),
            pltpu.VMEM((TILES, CH, LANES), BF16),
            pltpu.VMEM((TILES, CH, LANES), F32),
            pltpu.VMEM((TILES * SKEW, LANES), F32),
            pltpu.VMEM((ROWS, LANES), F32),
            pltpu.VMEM((ROWS, LANES), F32),
            pltpu.VMEM((2, CH, LANES), F32),
            pltpu.VMEM((2, 4 * CH, CH), BF16),
            pltpu.VMEM((2, CH, CH), BF16),
            pltpu.VMEM((2, CH, CH), BF16),
            pltpu.VMEM((8 * LANES, 8 * LANES), BF16),
            pltpu.VMEM((8 * LANES, 8 * LANES), BF16),
            pltpu.VMEM((8 * LANES, 8 * LANES), F32),
            pltpu.VMEM((CH, 1, LANES), F32),
            pltpu.VMEM((CH, GROUP, LANES), F32),
            pltpu.VMEM((CH, 32, LANES), F32),
            pltpu.VMEM((16, 56, LANES), F32),
            pltpu.VMEM((32, 56, LANES), F32),
            *messages,
            *messages,
            pltpu.SemaphoreType.DMA((16,)),
            pltpu.SemaphoreType.DMA((16,)),
            pltpu.SemaphoreType.DMA((2,)),
        ],
        compiler_params=pltpu.CompilerParams(
            collective_id=0, has_side_effects=True, vmem_limit_bytes=62 << 20
        ),
    )(pair_repr.reshape(flat_shape), *args)
    return out.reshape(pair_repr.shape)


def solution(mesh):
    in_specs = (P("row", "col", None), P(), P(), P(), P(), P(), P(), P(), P(), P())
    out_specs = P("row", "col", None)
    return jax.shard_map(body, mesh=mesh, in_specs=in_specs, out_specs=out_specs, check_vma=False)
```

time: 271 us -> 141 us (0.52)
  Pallas kernels: 0 us -> 138 us
  waiting for transfers between devices: 128 us -> 0 us
  local copies, waits for them, and re-layouts: 49.2 us -> 2.68 us
  starting transfers between devices: 39.8 us -> 0 us
  matrix products: 31.1 us -> 0 us
  other arithmetic: 21.7 us -> 0 us
    pallas_call x0 -> x1, Pallas kernels: none -> 138 us  [body(): pl.pallas_call(kernel, out_shape=jax.ShapeDtypeStruct(flat_shape, BF16),...]
    all_to_all x6 -> x0, waiting for transfers between devices: 128 us -> none  [the longest x2 45 us: triangle(): lax.all_to_all(left_op, ('row', 'col'), split_axis=0, concat_axis=1, tile...]
    all_to_all x6 -> x0, starting transfers between devices: 39.8 us -> none  [the longest x2 17.4 us: triangle(): lax.all_to_all(left_op, ('row', 'col'), split_axis=0, concat_axis=1, tile...]
    dot_general x8 -> x0, matrix products: 31.1 us -> none  [the longest x2 10.3 us: triangle(): jnp.einsum('ijc,cd->ijd', normed, w_gate, preferred_element_type=jnp.floa...]
    reduce_sum x7 -> x0, other arithmetic: 13.7 us -> none  [the longest x4 9.09 us: layer_norm(): spread = jnp.mean(center * center, axis=reduce_axes, keepdims=True)]
    convert_element_type x4 -> x0, local copies, waits for them, and re-layouts: 13.3 us -> none  [the longest x2 7.58 us: triangle(): right_op = (jax.nn.sigmoid(projected[2 * hidden:3 * hidden]) * projected[...]
    another operation x4 -> x0, local copies, waits for them, and re-layouts: 13 us -> none
    reshape x4 -> x0, local copies, waits for them, and re-layouts: 10.7 us -> none  [triangle(): product.reshape(per_dev, row_parts, row_count, col_parts, col_count)]
  transfers between devices with their start and end apart: 6 -> 0, of which waited for: 6 -> 0; matrix products, arithmetic and copies ran while one was open for 11% -> 0% of each run, Pallas kernels for 0% -> 0%
where the time goes in v3:
time: 141 us
  Pallas kernels  138 us (98%)
  local copies, waits for them, and re-layouts  2.68 us (2%)
    pallas_call x1, Pallas kernels, body(): pl.pallas_call(kernel, out_shape=jax.ShapeDtypeStruct(flat_shape, BF16),...  138 us

profile of v3, /device:TPU:1, one launch (start us, length us, event | category | flops | bytes accessed | tf_op | source)
XLA Modules:
  0.0 140.6 jit_solution(12441623113901040032)
XLA Ops:
  0.0 137.9 %shard_map.100 = bf16[6272,128]{1,0:T(8,128)(2,1)} custom-call(bf16[6272,128]{1,0:T(8,128)(2,1)} %bitcast.3, s32[896]{0:T(1024)} %mask_ref.1, s32[896]{0:T(1024)} %chain_ref.1, f32[2,128]{1,0:T(2,128)} %embed_ref.1, bf16[128,512]{1,0:T(8,128)(2,1)} %ab1_ref.1, bf16[128,128]{1,0:T(8,128)(2,1)} %gate1_ref.1, bf16[128,128]{1,0:T(8,128)(2,1)} %final1_ref.1, ...), custom_call_target="tpu_custom_call" | custom-call | tf_op jit(solution)/shard_map/pallas_call | solution.py:488
  137.9 2.7 %copy.12 = bf16[56,112,128]{2,1,0:T(8,128)(2,1)} copy(bf16[56,112,128]{2,1,0:T(8,128)(2,1)} %bitcast.2) | data formatting | bytes 3211264

commit v4 on v3

--- a/solution.py
+++ b/solution.py
@@ -19,9 +19,9 @@
 SHIFT = LANES - COLS
 SKEW = 136
 WIDE = 256
-FIRST = 24
-RA, RB, LA, LB, LX, PA, PB, PX = range(8)
-MESSAGES = (24, 24, 32, 16, 2, 24, 24, 2) + (24, 24, 24, 24, 2, 24, 24, 2)
+FIRST, SECOND = 24, 40
+RA, RL, LB, LX, PA, PB, PX, QA, QB, QC, QX, QPA, QPB, QPC, QPX = range(15)
+MESSAGES = (24, 56, 16, 2, 24, 24, 2) + (48, 32, 16, 2, 24, 16, 8, 2)
 
 
 def peer(step, row, col):
@@ -48,19 +48,33 @@
         one(step)
 
 
-def kernel(
-    x_hbm, mask_ref, chain_ref, embed_ref,
-    ab1_ref, gate1_ref, final1_ref, ab2_ref, gate2_ref, final2_ref,
-    out_ref,
-    x_ref, state, normed, gating, stage, pair_mask, same_chain, embed_t, ab_t, gate_t, final_t,
-    left_panel, right_panel, total, spare, kept, products, flat, flat_product,
-    *rest,
-):
-    outs, ins = rest[:16], rest[16:32]
-    send_sem, recv_sem, x_sem = rest[32:]
+def kernel(*refs):
+    inputs, (out_hbm, *refs) = refs[:10], refs[10:]
+    here, refs = refs[:10], refs[10:]
+    x_ref, mask_ref, chain_ref, embed_ref, ab1_ref, gate1_ref, final1_ref, ab2_ref, gate2_ref, final2_ref = here
+    out_ref, state, normed, gating, left_stage, right_stage, pair_mask, same_chain, embed_t, ab_t, gate_t, final_t, *refs = refs
+    left_panel, right_panel, total, kept, products, flat, flat_product, *refs = refs
+    LEFT, RIGHT = 0, 1
+    stages = left_stage, right_stage
+    count = len(MESSAGES)
+    outs, ins = refs[:count], refs[count : 2 * count]
+    send_sem, recv_sem, in_sem, out_sem = refs[2 * count :]
     row, col = lax.axis_index("row"), lax.axis_index("col")
     me = row * 8 + col
     barrier = pltpu.get_barrier_semaphore()
+
+    copies = {}
+    for name, k in (("mask", 1), ("chain", 2), ("embed", 3), ("ab1", 4)):
+        copies[name] = pltpu.make_async_copy(inputs[k], here[k], in_sem.at[k])
+        copies[name].start()
+    x_copies, out_copies = [], []
+    for number, (begin, end) in enumerate(((0, FIRST), (FIRST, TILES))):
+        at = pl.ds(begin * LANES, (end - begin) * LANES)
+        x_copies.append(pltpu.make_async_copy(inputs[0].at[at], x_ref.at[at], in_sem.at[10 * number]))
+        x_copies[number].start()
+    for number, (begin, end) in enumerate(((0, FIRST), (FIRST, SECOND), (SECOND, TILES))):
+        at = pl.ds(begin * LANES, (end - begin) * LANES)
+        out_copies.append(pltpu.make_async_copy(out_ref.at[at], out_hbm.at[at], out_sem.at[number]))
 
     def greet(row_to, col_to):
         pl.semaphore_signal(barrier, inc=1, device_id=(row_to, col_to), device_id_type=MESH)
@@ -73,11 +87,9 @@
     for k in range(1, 8):
         greet(row, lax.rem(col + k, 8))
     lax.fori_loop(1, 16, greet_row, 0)
-    x_copies = []
-    for number, (begin, end) in enumerate(((0, FIRST * LANES), (FIRST * LANES, TILES * LANES))):
-        at = pl.ds(begin, end - begin)
-        x_copies.append(pltpu.make_async_copy(x_hbm.at[at], x_ref.at[at], x_sem.at[number]))
-        x_copies[number].start()
+    for name, k in (("gate1", 5), ("final1", 6), ("ab2", 7), ("gate2", 8), ("final2", 9)):
+        copies[name] = pltpu.make_async_copy(inputs[k], here[k], in_sem.at[k])
+        copies[name].start()
 
     def turned(value):
         return value.astype(F32).T.astype(BF16)
@@ -86,6 +98,8 @@
         for part in (2 * side, 2 * side + 1):
             ab_t[update, part * CH : (part + 1) * CH, :] = turned(ab[:, part * CH : (part + 1) * CH])
 
+    copies["mask"].wait()
+    copies["chain"].wait()
     lane = lax.broadcasted_iota(jnp.int32, (1, LANES), 1)
 
     def collect(j, carry):
@@ -148,7 +162,7 @@
         both = jnp.dot(weights, jnp.concatenate(units, axis=1), preferred_element_type=F32)
         for k, t in enumerate(tiles):
             one = both[:, k * LANES : (k + 1) * LANES]
-            stage[tile_at(t), :] = sigmoid(one[:CH]) * one[CH:] * pair_mask[pl.ds(t, 1), :]
+            stages[side][tile_at(t), :] = sigmoid(one[:CH]) * one[CH:] * pair_mask[pl.ds(t, 1), :]
 
     def for_tiles(begin, end, visit):
         def turn(n, carry):
@@ -159,8 +173,6 @@
         lax.fori_loop(0, turns, turn, 0)
         if begin + turns * 4 < end:
             visit(list(range(begin + turns * 4, end)))
-
-    LEFT, RIGHT = 0, 1
 
     def send(number, row_to, col_to):
         pltpu.make_async_remote_copy(
@@ -168,8 +180,8 @@
             send_sem.at[number], recv_sem.at[number], device_id=(row_to, col_to), device_id_type=MESH,
         ).start()
 
-    def staged(channel, begin, count):
-        return stage[pl.ds(begin * SKEW + channel, count, stride=SKEW), :]
+    def staged(side, channel, begin, count):
+        return stages[side][pl.ds(begin * SKEW + channel, count, stride=SKEW), :]
 
     def relay(make):
         def one(step):
@@ -223,15 +235,11 @@
             at = 7 * (begin + g)
             flat_product[slot, at : at + GROUP] = fold(rows[g * GROUP : (g + 1) * GROUP])
 
-    def mix(update, half):
-        begin, count, padded = ((0, FIRST, FIRST), (FIRST, TILES - FIRST, 32))[half]
-        pa, pb, px = (update * 8 + number for number in (PA, PB, PX))
+    def mix(begin, count, tile_of):
+        padded = -(-count // GROUP) * GROUP
 
         def add(c, carry):
-            if half == 0:
-                tile = got(pa, c)
-            else:
-                tile = jnp.concatenate([got(pb, c), jnp.broadcast_to(got(px, c)[0:1], (GROUP, LANES))], axis=0)
+            tile = tile_of(c)
             products[c, :padded] = tile
             return carry + tile
 
@@ -247,26 +255,30 @@
 
         def put(c, carry):
             value = (products[c, :padded] - mean) * scale
-            stage[pl.ds(begin * SKEW + c, count, stride=SKEW), :] = value[:count]
+            left_stage[pl.ds(begin * SKEW + c, count, stride=SKEW), :] = value[:count]
             return carry
 
         lax.fori_loop(0, CH, put, 0, unroll=8)
 
+    def got_with_row(number, extra, c):
+        return jnp.concatenate([got(number, c), jnp.broadcast_to(got(extra, c)[0:1], (GROUP, LANES))], axis=0)
+
     def changed(update, tiles):
-        mixed = jnp.concatenate([stage[tile_at(t), :].astype(BF16) for t in tiles], axis=1)
+        mixed = jnp.concatenate([left_stage[tile_at(t), :].astype(BF16) for t in tiles], axis=1)
         change = jnp.dot(final_t[update], mixed, preferred_element_type=F32)
         return [
             state[t] + gating[t] * change[:, k * LANES : (k + 1) * LANES] for k, t in enumerate(tiles)
         ]
 
-    def first(update):
+    def first(update, sides):
         def visit(tiles):
             values = [start_state(t) for t in tiles] if update == 0 else changed(0, tiles)
             units = [norm(value) for value in values]
             for t, value, unit in zip(tiles, values, units):
                 state[t] = value
                 normed[t] = unit
-            operand(update, RIGHT, tiles, units)
+            for side in sides:
+                operand(update, side, tiles, units)
 
         return visit
 
@@ -289,36 +301,36 @@
         for t, value in zip(tiles, changed(1, tiles)):
             out_ref[positions(t), :] = value.T.astype(BF16)
 
+    copies["ab1"].wait()
     turn_ab(0, ab1_ref, RIGHT)
+    copies["embed"].wait()
     for kind in range(2):
         embed_t[kind] = jnp.broadcast_to(embed_ref[kind : kind + 1, :], (CH, CH)).T
     x_copies[0].wait()
-    for_tiles(0, FIRST, first(0))
-
-    def right_first(channel):
-        return [(RA, staged(channel, 0, FIRST))]
-
-    def right_second(channel):
-        spare[channel] = staged(channel, TILES - 1, 1)
-        return [(RB, staged(channel, FIRST, 24))]
-
-    def left_first(channel):
-        tile = staged(channel, 0, 32)
-        end = jnp.where(row_of == 7, jnp.broadcast_to(spare[channel], (GROUP, LANES)), tile[24:])
-        return [(LA, jnp.concatenate([tile[:24], end], axis=0))]
-
-    def left_second(channel):
-        return [(LB, staged(channel, 31, 16)), (LX, staged(channel, 47, 2))]
+    for_tiles(0, FIRST, first(0, [RIGHT]))
+
+    def right_early(channel):
+        return [(RA, staged(RIGHT, channel, 0, FIRST))]
+
+    def right_left(channel):
+        tile = staged(LEFT, channel, 0, 32)
+        last_right = jnp.broadcast_to(staged(RIGHT, channel, TILES - 1, 1), (GROUP, LANES))
+        end = jnp.where(row_of == 7, last_right, tile[24:])
+        return [(RL, jnp.concatenate([staged(RIGHT, channel, FIRST, 24), tile[:24], end], axis=0))]
+
+    def left_late(channel):
+        return [(LB, staged(LEFT, channel, 31, 16)), (LX, staged(LEFT, channel, 47, 2))]
 
     pl.semaphore_wait(barrier, 127)
-    relay(right_first)
+    relay(right_early)
+    turn_ab(0, ab1_ref, LEFT)
     x_copies[1].wait()
-    for_tiles(FIRST, TILES, first(0))
-    relay(right_second)
-    turn_ab(0, ab1_ref, LEFT)
-    for_tiles(0, TILES, second(0))
-    relay(left_first)
-    relay(left_second)
+    for_tiles(FIRST, TILES, first(0, [RIGHT, LEFT]))
+    for_tiles(0, FIRST, second(0))
+    relay(right_left)
+    relay(left_late)
+    for name in ("gate1", "final1", "ab2", "gate2", "final2"):
+        copies[name].wait()
     for update, (gate, final) in enumerate(((gate1_ref, final1_ref), (gate2_ref, final2_ref))):
         gate_t[update] = turned(gate[...])
         final_t[update] = turned(final[...])
@@ -330,9 +342,10 @@
         empty = jnp.zeros((LANES - 2 * ROWS, LANES), F32)
         for r in range(16):
             source = r * 8 + s
+            both = got(RL, source)
             flat[r, 0:24] = got(RA, source)
-            flat[r, 24:48] = got(RB, source)
-            flat[r, 48:49] = got(LA, source)[31:32]
+            flat[r, 24:48] = both[:24]
+            flat[r, 48:49] = both[55:]
         for a in range(8):
             rows = unfolded(2 * a, 0, 7) + unfolded(2 * a + 1, 0, 7)
             rows = [jnp.where(lanes < COLS, part, 0.0) for part in rows]
@@ -341,7 +354,7 @@
     def left_columns_first(s, at):
         rows = []
         for r in range(16):
-            flat[r, 0:32] = got(LA, r * 8 + s)
+            flat[r, 0:32] = got(RL, r * 8 + s)[24:]
             rows += unfolded(r, 0, 4)
         left_panel[:512, at] = jnp.concatenate(rows, axis=0).astype(BF16)
 
@@ -349,7 +362,7 @@
         rows = []
         for r in range(16):
             source = r * 8 + s
-            flat[r, 24:32] = got(LA, source)[24:32]
+            flat[r, 24:32] = got(RL, source)[48:]
             flat[r, 31:47] = got(LB, source)
             flat[r, 47:49] = got(LX, source)
             rows += unfolded(r, 4, 7)
@@ -380,7 +393,7 @@
 
         wide(visit)
 
-    arrive(RA, RB, LA)
+    arrive(RA, RL)
     columns(right_columns)
     columns(left_columns_first)
     outgoing_product(0, 512, 0)
@@ -390,111 +403,132 @@
     outgoing_product(512, 896, 1)
     give(PB, PX)
 
-    def right_one(channel):
-        return [(8 + RA, staged(channel, 0, FIRST))]
-
-    def left_one(channel):
-        return [(8 + LA, staged(channel, 0, FIRST))]
-
-    def right_two(channel):
-        spare[channel] = staged(channel, TILES - 1, 1)
-        return [(8 + RB, staged(channel, FIRST, 24))]
-
-    def left_two(channel):
-        extra = jnp.concatenate([spare[channel], staged(channel, TILES - 1, 1)], axis=0)
-        return [(8 + LB, staged(channel, FIRST, 24)), (8 + LX, extra)]
+    def both(number, begin, count):
+        return lambda channel: [
+            (number, jnp.concatenate([staged(side, channel, begin, count) for side in (RIGHT, LEFT)], axis=0))
+        ]
+
+    def rest(channel):
+        extra = [staged(side, channel, TILES - 1, 1) for side in (RIGHT, LEFT)]
+        return both(QC, SECOND, 8)(channel) + [(QX, jnp.concatenate(extra, axis=0))]
 
     arrive(PA)
-    mix(0, 0)
-    for_tiles(0, FIRST, first(1))
-    relay(right_one)
-    for_tiles(0, FIRST, second(1))
-    relay(left_one)
+    mix(0, 24, lambda c: got(PA, c))
+    for_tiles(0, FIRST, first(1, [RIGHT, LEFT]))
+    relay(both(QA, 0, FIRST))
     arrive(PB, PX)
-    mix(0, 1)
-    for_tiles(FIRST, TILES, first(1))
-    relay(right_two)
-    for_tiles(FIRST, TILES, second(1))
-    relay(left_two)
-    for_tiles(0, TILES, third(1))
-
-    def incoming_columns(begin, end, numbers, turn):
-        first_group, last_group = begin // GROUP, end // GROUP
+    mix(24, 25, lambda c: got_with_row(PB, PX, c))
+    for_tiles(FIRST, SECOND, first(1, [RIGHT, LEFT]))
+    relay(both(QB, FIRST, 16))
+    for_tiles(SECOND, TILES, first(1, [RIGHT, LEFT]))
+    relay(rest)
+
+    def incoming_columns(begin, end, numbers):
         depth = pl.ds(16 * begin, 16 * (end - begin))
 
         def visit(s, at):
-            rows = []
+            both_rows = [], []
             for r in range(16):
                 source = r * 8 + s
-                flat[r, 0:24] = got(numbers[0], source)
-                if end == ROWS:
-                    flat[r, 24:48] = got(numbers[1], source)
-                    extra = got(8 + LX, source)
-                    flat[r, 48:49] = extra[1:2] if turn else extra[0:1]
-                rows += unfolded(r, first_group, last_group)
-            rows = jnp.concatenate(rows, axis=0)
-            if turn:
-                left_panel[at, depth] = rows.T.astype(BF16)
-            else:
-                right_panel[depth, at] = rows.astype(BF16)
+                for k, side in enumerate((RIGHT, LEFT)):
+                    slot = r + 16 * k
+                    for top, number in numbers:
+                        count = MESSAGES[number] // 2
+                        if number == QX:
+                            flat[slot, top : top + 1] = got(QX, source)[k : k + 1]
+                        else:
+                            flat[slot, top : top + count] = got(number, source)[k * count : (k + 1) * count]
+                    both_rows[k].extend(unfolded(slot, begin // GROUP, end // GROUP))
+            right_panel[depth, at] = jnp.concatenate(both_rows[0], axis=0).astype(BF16)
+            left_panel[at, depth] = jnp.concatenate(both_rows[1], axis=0).T.astype(BF16)
 
         columns(visit)
 
+    def incoming_part(begin, end, at):
+        return jnp.dot(left_panel[:, begin:end], right_panel[begin:end, at], preferred_element_type=F32)
+
     def incoming_first(n, at):
-        total[:, at] = jnp.dot(left_panel[:, :384], right_panel[:384, at], preferred_element_type=F32)
+        total[:, at] = incoming_part(0, 384, at)
 
     def incoming_second(n, at):
-        part = total[:, at] + jnp.dot(
-            left_panel[:, 384:896], right_panel[384:896, at], preferred_element_type=F32
-        )
+        total[:, at] += incoming_part(384, 640, at)
+
+    def incoming_third(turn, carry):
+        n = lax.rem(turn + row, 4)
+        at = pl.ds(pl.multiple_of(n * WIDE, WIDE), WIDE)
+        part = total[:, at] + incoming_part(640, 896, at)
         for r in range(16):
             top = (r // 2) * LANES + (r % 2) * ROWS
             for k in range(WIDE // LANES):
                 dest = r * 8 + n * (WIDE // LANES) + k
                 slot = r * 2 + k
                 folded(slot, 0, part[top : top + ROWS, k * LANES : (k + 1) * LANES])
-                outs[8 + PA][dest] = flat_product[slot, 0:24].astype(BF16)
-                outs[8 + PB][dest] = flat_product[slot, 24:48].astype(BF16)
-                outs[8 + PX][dest] = flat_product[slot, 48:50].astype(BF16)
-
-    rights, lefts = (8 + RA, 8 + RB), (8 + LA, 8 + LB)
-    arrive(8 + RA)
-    incoming_columns(0, 24, rights, False)
-    arrive(8 + LA)
-    incoming_columns(0, 24, lefts, True)
+                outs[QPA][dest] = flat_product[slot, 0:24].astype(BF16)
+                outs[QPB][dest] = flat_product[slot, 24:40].astype(BF16)
+                outs[QPC][dest] = flat_product[slot, 40:48].astype(BF16)
+                outs[QPX][dest] = flat_product[slot, 48:50].astype(BF16)
+        for i in range(16):
+            for k in range(WIDE // LANES):
+                row_to = lax.rem(row + 5 * i, 16)
+                col_to = n * (WIDE // LANES) + lax.rem(col + k, 2)
+                if i == 0 and k == 0:
+                    pl.when(row_to * 8 + col_to != me)(lambda: send(QPA, row_to, col_to))
+                else:
+                    send(QPA, row_to, col_to)
+        return carry
+
+    arrive(QA)
+    incoming_columns(0, 24, [(0, QA)])
     wide(incoming_first)
-    arrive(8 + RB, 8 + LB, 8 + LX)
-    incoming_columns(24, 56, rights, False)
-    incoming_columns(24, 56, lefts, True)
+    arrive(QB)
+    incoming_columns(24, 40, [(0, QA), (24, QB)])
     wide(incoming_second)
-    give(8 + PA)
-    give(8 + PB, 8 + PX)
-    arrive(8 + PA)
-    mix(1, 0)
+    arrive(QC, QX)
+    incoming_columns(40, 56, [(24, QB), (40, QC), (48, QX)])
+    lax.fori_loop(0, 4, incoming_third, 0)
+    ins[QPA][me] = outs[QPA][me]
+    give(QPB)
+    give(QPC, QPX)
+    for_tiles(0, TILES, third(1))
+
+    arrive(QPA)
+    mix(0, 24, lambda c: got(QPA, c))
     for_tiles(0, FIRST, last)
-    arrive(8 + PB, 8 + PX)
-    mix(1, 1)
-    for_tiles(FIRST, TILES, last)
-
-    for number in range(16):
+    out_copies[0].start()
+    arrive(QPB)
+    mix(24, 16, lambda c: got(QPB, c))
+    for_tiles(FIRST, SECOND, last)
+    out_copies[1].start()
+    arrive(QPC, QPX)
+    mix(40, 9, lambda c: got_with_row(QPC, QPX, c))
+    for_tiles(SECOND, TILES, last)
+    out_copies[2].start()
+
+    for number in range(len(MESSAGES)):
         others = outs[number].at[pl.ds(0, 127)]
         pltpu.make_async_copy(others, others, send_sem.at[number]).wait()
+    for copy in out_copies:
+        copy.wait()
 
 
 def body(pair_repr, *args):
-    vmem, smem = (pl.BlockSpec(memory_space=m) for m in (pltpu.VMEM, pltpu.SMEM))
     messages = [pltpu.VMEM((CH, count, LANES), BF16) for count in MESSAGES]
     flat_shape = (TILES * LANES, CH)
+    held = [pltpu.VMEM(flat_shape, BF16)]
+    for number, arg in enumerate(args):
+        held.append((pltpu.SMEM if number < 2 else pltpu.VMEM)(arg.shape, arg.dtype))
     out = pl.pallas_call(
         kernel,
-        out_shape=jax.ShapeDtypeStruct(flat_shape, BF16),
-        in_specs=[pl.BlockSpec(memory_space=pl.ANY), smem, smem] + [vmem] * 7,
-        out_specs=vmem,
+        out_shape=pltpu.VMEM(flat_shape, BF16),
+        in_specs=[pl.BlockSpec(memory_space=pltpu.HBM)] * 10,
+        out_specs=pl.BlockSpec(memory_space=pl.ANY),
         scratch_shapes=[
+            *held,
             pltpu.VMEM(flat_shape, BF16),
             pltpu.VMEM((TILES, CH, LANES), F32),
             pltpu.VMEM((TILES, CH, LANES), BF16),
             pltpu.VMEM((TILES, CH, LANES), F32),
+            pltpu.VMEM((TILES * SKEW, LANES), F32),
             pltpu.VMEM((TILES * SKEW, LANES), F32),
             pltpu.VMEM((ROWS, LANES), F32),
             pltpu.VMEM((ROWS, LANES), F32),
@@ -505,21 +539,21 @@
             pltpu.VMEM((8 * LANES, 8 * LANES), BF16),
             pltpu.VMEM((8 * LANES, 8 * LANES), BF16),
             pltpu.VMEM((8 * LANES, 8 * LANES), F32),
-            pltpu.VMEM((CH, 1, LANES), F32),
             pltpu.VMEM((CH, GROUP, LANES), F32),
             pltpu.VMEM((CH, 32, LANES), F32),
-            pltpu.VMEM((16, 56, LANES), F32),
+            pltpu.VMEM((32, 56, LANES), F32),
             pltpu.VMEM((32, 56, LANES), F32),
             *messages,
             *messages,
-            pltpu.SemaphoreType.DMA((16,)),
-            pltpu.SemaphoreType.DMA((16,)),
-            pltpu.SemaphoreType.DMA((2,)),
+            pltpu.SemaphoreType.DMA((len(MESSAGES),)),
+            pltpu.SemaphoreType.DMA((len(MESSAGES),)),
+            pltpu.SemaphoreType.DMA((11,)),
+            pltpu.SemaphoreType.DMA((3,)),
         ],
         compiler_params=pltpu.CompilerParams(
-            collective_id=0, has_side_effects=True, vmem_limit_bytes=62 << 20
+            collective_id=0, has_side_effects=True, vmem_limit_bytes=56 << 20
         ),
-    )(pair_repr.reshape(flat_shape), *args)
+    )(*(pltpu.with_memory_space_constraint(a, pltpu.HBM) for a in (pair_repr.reshape(flat_shape), *args)))
     return out.reshape(pair_repr.shape)
 
 

time: 141 us -> 137 us (0.972)
  Pallas kernels: 138 us -> 136 us
  local copies, waits for them, and re-layouts: 2.68 us -> 1.16 us
    pallas_call x1, Pallas kernels: 138 us -> 136 us  [body(): pl.pallas_call(kernel, out_shape=pltpu.VMEM(flat_shape, BF16), in_specs=[...]
    unnamed x1, local copies, waits for them, and re-layouts: 2.68 us -> 1.16 us
where the time goes in v4:
time: 137 us
  Pallas kernels  136 us (99%)
    pallas_call x1, Pallas kernels, body(): pl.pallas_call(kernel, out_shape=pltpu.VMEM(flat_shape, BF16), in_specs=[...  136 us

profile of v4, /device:TPU:1, one launch (start us, length us, event | category | flops | bytes accessed | tf_op | source)
XLA Modules:
  0.0 136.9 jit_solution(12541039251114387716)
XLA Ops:
  0.0 135.8 %shard_map.100 = bf16[6272,128]{1,0:T(8,128)(2,1)S(1)} custom-call(bf16[6272,128]{1,0:T(8,128)(2,1)} %bitcast.3, s32[896]{0:T(1024)} %refs_1_.1, s32[896]{0:T(1024)} %refs_2_.1, f32[2,128]{1,0:T(2,128)} %refs_3_.1, bf16[128,512]{1,0:T(8,128)(2,1)} %refs_4_.1, bf16[128,128]{1,0:T(8,128)(2,1)} %refs_5_.1, bf16[128,128]{1,0:T(8,128)(2,1)} %refs_6_.1, ...), custom_call_target="tpu_custom_call" | custom-call | tf_op jit(solution)/shard_map/pallas_call | solution.py:520
  135.8 1.2 copy.12

commit v5 on v4

--- a/solution.py
+++ b/solution.py
@@ -20,8 +20,8 @@
 SKEW = 136
 WIDE = 256
 FIRST, SECOND = 24, 40
-RA, RL, LB, LX, PA, PB, PX, QA, QB, QC, QX, QPA, QPB, QPC, QPX = range(15)
-MESSAGES = (24, 56, 16, 2, 24, 24, 2) + (48, 32, 16, 2, 24, 16, 8, 2)
+RA, RB, LA, LB, LX, PA, PB, PX, QA, QB, QC, QX, QPA, QPB, QPC, QPX = range(16)
+MESSAGES = (24, 24, 32, 16, 2, 24, 24, 2) + (48, 32, 16, 2, 24, 16, 8, 2)
 
 
 def peer(step, row, col):
@@ -227,6 +227,23 @@
 
         lax.fori_loop(0, 8 * LANES // WIDE, turn, 0)
 
+    def wide_and_send(visit, number):
+        def turn(n, carry):
+            n = lax.rem(n + row, 8 * LANES // WIDE)
+            visit(n, pl.ds(pl.multiple_of(n * WIDE, WIDE), WIDE))
+            for i in range(16):
+                for k in range(WIDE // LANES):
+                    row_to = lax.rem(row + 5 * i, 16)
+                    col_to = n * (WIDE // LANES) + lax.rem(col + k, 2)
+                    if i == 0 and k == 0:
+                        pl.when(row_to * 8 + col_to != me)(lambda: send(number, row_to, col_to))
+                    else:
+                        send(number, row_to, col_to)
+            return carry
+
+        lax.fori_loop(0, 8 * LANES // WIDE, turn, 0)
+        ins[number][me] = outs[number][me]
+
     def unfolded(r, begin, end):
         return [unfold(flat[r, 7 * g : 7 * g + GROUP]) for g in range(begin, end)]
 
@@ -312,22 +329,26 @@
     def right_early(channel):
         return [(RA, staged(RIGHT, channel, 0, FIRST))]
 
-    def right_left(channel):
+    def right_late(channel):
+        return [(RB, staged(RIGHT, channel, FIRST, 24))]
+
+    def left_early(channel):
         tile = staged(LEFT, channel, 0, 32)
         last_right = jnp.broadcast_to(staged(RIGHT, channel, TILES - 1, 1), (GROUP, LANES))
         end = jnp.where(row_of == 7, last_right, tile[24:])
-        return [(RL, jnp.concatenate([staged(RIGHT, channel, FIRST, 24), tile[:24], end], axis=0))]
+        return [(LA, jnp.concatenate([tile[:24], end], axis=0))]
 
     def left_late(channel):
         return [(LB, staged(LEFT, channel, 31, 16)), (LX, staged(LEFT, channel, 47, 2))]
 
     pl.semaphore_wait(barrier, 127)
     relay(right_early)
+    x_copies[1].wait()
+    for_tiles(FIRST, TILES, first(0, [RIGHT]))
+    relay(right_late)
     turn_ab(0, ab1_ref, LEFT)
-    x_copies[1].wait()
-    for_tiles(FIRST, TILES, first(0, [RIGHT, LEFT]))
-    for_tiles(0, FIRST, second(0))
-    relay(right_left)
+    for_tiles(0, TILES, second(0))
+    relay(left_early)
     relay(left_late)
     for name in ("gate1", "final1", "ab2", "gate2", "final2"):
         copies[name].wait()
@@ -338,23 +359,32 @@
         turn_ab(1, ab2_ref, side)
     for_tiles(0, TILES, third(0))
 
-    def right_columns(s, at):
-        empty = jnp.zeros((LANES - 2 * ROWS, LANES), F32)
+    def right_columns_most(s, at):
         for r in range(16):
             source = r * 8 + s
-            both = got(RL, source)
             flat[r, 0:24] = got(RA, source)
-            flat[r, 24:48] = both[:24]
-            flat[r, 48:49] = both[55:]
+            flat[r, 24:48] = got(RB, source)
+            rows = [jnp.where(lanes < COLS, part, 0.0) for part in unfolded(r, 0, 6)]
+            top = (r // 2) * LANES + (r % 2) * ROWS
+            total[top : top + 48, at] = jnp.concatenate(rows, axis=0)
+
+    def right_columns(s, at):
+        rows = []
+        for r in range(16):
+            source = r * 8 + s
+            flat[r, 40:48] = got(RB, source)[16:]
+            flat[r, 48:49] = got(LA, source)[31:]
+            top = (r // 2) * LANES + (r % 2) * ROWS
+            rows += [total[top : top + 48, at], jnp.where(lanes < COLS, unfolded(r, 6, 7)[0], 0.0)]
+        empty = jnp.zeros((LANES - 2 * ROWS, LANES), F32)
         for a in range(8):
-            rows = unfolded(2 * a, 0, 7) + unfolded(2 * a + 1, 0, 7)
-            rows = [jnp.where(lanes < COLS, part, 0.0) for part in rows]
-            right_panel[a * LANES : (a + 1) * LANES, at] = jnp.concatenate(rows + [empty], axis=0).astype(BF16)
+            panel = jnp.concatenate(rows[4 * a : 4 * a + 4] + [empty], axis=0)
+            right_panel[a * LANES : (a + 1) * LANES, at] = panel.astype(BF16)
 
     def left_columns_first(s, at):
         rows = []
         for r in range(16):
-            flat[r, 0:32] = got(RL, r * 8 + s)[24:]
+            flat[r, 0:32] = got(LA, r * 8 + s)
             rows += unfolded(r, 0, 4)
         left_panel[:512, at] = jnp.concatenate(rows, axis=0).astype(BF16)
 
@@ -362,7 +392,7 @@
         rows = []
         for r in range(16):
             source = r * 8 + s
-            flat[r, 24:32] = got(RL, source)[48:]
+            flat[r, 24:32] = got(LA, source)[24:]
             flat[r, 31:47] = got(LB, source)
             flat[r, 47:49] = got(LX, source)
             rows += unfolded(r, 4, 7)
@@ -391,13 +421,17 @@
                         outs[PB][dest] = flat_product[slot, 24:48].astype(BF16)
                         outs[PX][dest] = flat_product[slot, 48:50].astype(BF16)
 
-        wide(visit)
-
-    arrive(RA, RL)
+        if half == 0:
+            wide_and_send(visit, PA)
+        else:
+            wide(visit)
+
+    arrive(RA, RB)
+    columns(right_columns_most)
+    arrive(LA)
     columns(right_columns)
     columns(left_columns_first)
     outgoing_product(0, 512, 0)
-    give(PA)
     arrive(LB, LX)
     columns(left_columns_second)
     outgoing_product(512, 896, 1)
@@ -453,9 +487,7 @@
     def incoming_second(n, at):
         total[:, at] += incoming_part(384, 640, at)
 
-    def incoming_third(turn, carry):
-        n = lax.rem(turn + row, 4)
-        at = pl.ds(pl.multiple_of(n * WIDE, WIDE), WIDE)
+    def incoming_third(n, at):
         part = total[:, at] + incoming_part(640, 896, at)
         for r in range(16):
             top = (r // 2) * LANES + (r % 2) * ROWS
@@ -467,15 +499,6 @@
                 outs[QPB][dest] = flat_product[slot, 24:40].astype(BF16)
                 outs[QPC][dest] = flat_product[slot, 40:48].astype(BF16)
                 outs[QPX][dest] = flat_product[slot, 48:50].astype(BF16)
-        for i in range(16):
-            for k in range(WIDE // LANES):
-                row_to = lax.rem(row + 5 * i, 16)
-                col_to = n * (WIDE // LANES) + lax.rem(col + k, 2)
-                if i == 0 and k == 0:
-                    pl.when(row_to * 8 + col_to != me)(lambda: send(QPA, row_to, col_to))
-                else:
-                    send(QPA, row_to, col_to)
-        return carry
 
     arrive(QA)
     incoming_columns(0, 24, [(0, QA)])
@@ -485,8 +508,7 @@
     wide(incoming_second)
     arrive(QC, QX)
     incoming_columns(40, 56, [(24, QB), (40, QC), (48, QX)])
-    lax.fori_loop(0, 4, incoming_third, 0)
-    ins[QPA][me] = outs[QPA][me]
+    wide_and_send(incoming_third, QPA)
     give(QPB)
     give(QPC, QPX)
     for_tiles(0, TILES, third(1))

time: 137 us -> 132 us (0.964)
  Pallas kernels: 136 us -> 130 us
    pallas_call x1, Pallas kernels: 136 us -> 130 us  [body(): pl.pallas_call(kernel, out_shape=pltpu.VMEM(flat_shape, BF16), in_specs=[...]
where the time goes in v5:
time: 132 us; the launch traced here: 131 us
  Pallas kernels  130 us (98%)
    pallas_call x1, Pallas kernels, body(): pl.pallas_call(kernel, out_shape=pltpu.VMEM(flat_shape, BF16), in_specs=[...  130 us

profile of v5, /device:TPU:1, one launch (start us, length us, event | category | flops | bytes accessed | tf_op | source)
XLA Modules:
  0.0 131.2 jit_solution(12267910204103056595)
XLA Ops:
  0.0 130.0 %shard_map.100 = bf16[6272,128]{1,0:T(8,128)(2,1)S(1)} custom-call(bf16[6272,128]{1,0:T(8,128)(2,1)} %bitcast.3, s32[896]{0:T(1024)} %refs_1_.1, s32[896]{0:T(1024)} %refs_2_.1, f32[2,128]{1,0:T(2,128)} %refs_3_.1, bf16[128,512]{1,0:T(8,128)(2,1)} %refs_4_.1, bf16[128,128]{1,0:T(8,128)(2,1)} %refs_5_.1, bf16[128,128]{1,0:T(8,128)(2,1)} %refs_6_.1, ...), custom_call_target="tpu_custom_call" | custom-call | tf_op jit(solution)/shard_map/pallas_call | solution.py:542
  130.0 1.2 copy.12

commit v6 on v5

--- a/solution.py
+++ b/solution.py
@@ -20,12 +20,12 @@
 SKEW = 136
 WIDE = 256
 FIRST, SECOND = 24, 40
-RA, RB, LA, LB, LX, PA, PB, PX, QA, QB, QC, QX, QPA, QPB, QPC, QPX = range(16)
-MESSAGES = (24, 24, 32, 16, 2, 24, 24, 2) + (48, 32, 16, 2, 24, 16, 8, 2)
+RA, RB, LA, LB, LX, PA, PB, PX, QRA, QLA, QB, QC, QX, QPA, QPB, QPC, QPX = range(17)
+MESSAGES = (24, 24, 32, 16, 2, 24, 24, 2) + (24, 24, 32, 16, 2, 24, 16, 8, 2)
 
 
 def peer(step, row, col):
-    far = lax.rem(37 * step, 128)
+    far = lax.rem(59 * step, 128)
     core = lax.rem(row + far, 2)
     x = lax.rem(row // 2 + far // 2, 4)
     z = lax.rem(col + far // 8, 4)
@@ -448,8 +448,10 @@
 
     arrive(PA)
     mix(0, 24, lambda c: got(PA, c))
-    for_tiles(0, FIRST, first(1, [RIGHT, LEFT]))
-    relay(both(QA, 0, FIRST))
+    for_tiles(0, FIRST, first(1, [RIGHT]))
+    relay(lambda channel: [(QRA, staged(RIGHT, channel, 0, FIRST))])
+    for_tiles(0, FIRST, second(1))
+    relay(lambda channel: [(QLA, staged(LEFT, channel, 0, FIRST))])
     arrive(PB, PX)
     mix(24, 25, lambda c: got_with_row(PB, PX, c))
     for_tiles(FIRST, SECOND, first(1, [RIGHT, LEFT]))
@@ -470,6 +472,8 @@
                         count = MESSAGES[number] // 2
                         if number == QX:
                             flat[slot, top : top + 1] = got(QX, source)[k : k + 1]
+                        elif number == QRA:
+                            flat[slot, top : top + FIRST] = got((QRA, QLA)[k], source)
                         else:
                             flat[slot, top : top + count] = got(number, source)[k * count : (k + 1) * count]
                     both_rows[k].extend(unfolded(slot, begin // GROUP, end // GROUP))
@@ -500,11 +504,11 @@
                 outs[QPC][dest] = flat_product[slot, 40:48].astype(BF16)
                 outs[QPX][dest] = flat_product[slot, 48:50].astype(BF16)
 
-    arrive(QA)
-    incoming_columns(0, 24, [(0, QA)])
+    arrive(QRA, QLA)
+    incoming_columns(0, 24, [(0, QRA)])
     wide(incoming_first)
     arrive(QB)
-    incoming_columns(24, 40, [(0, QA), (24, QB)])
+    incoming_columns(24, 40, [(0, QRA), (24, QB)])
     wide(incoming_second)
     arrive(QC, QX)
     incoming_columns(40, 56, [(24, QB), (40, QC), (48, QX)])

time: 132 us -> 130 us (0.985)
  no operation moved by 1% of the time
where the time goes in v6:
time: 130 us
  Pallas kernels  129 us (99%)
    pallas_call x1, Pallas kernels, body(): pl.pallas_call(kernel, out_shape=pltpu.VMEM(flat_shape, BF16), in_specs=[...  129 us

profile of v6, /device:TPU:1, one launch (start us, length us, event | category | flops | bytes accessed | tf_op | source)
XLA Modules:
  0.0 130.4 jit_solution(17692478811848926966)
XLA Ops:
  0.0 129.2 %shard_map.100 = bf16[6272,128]{1,0:T(8,128)(2,1)S(1)} custom-call(bf16[6272,128]{1,0:T(8,128)(2,1)} %bitcast.3, s32[896]{0:T(1024)} %refs_1_.1, s32[896]{0:T(1024)} %refs_2_.1, f32[2,128]{1,0:T(2,128)} %refs_3_.1, bf16[128,512]{1,0:T(8,128)(2,1)} %refs_4_.1, bf16[128,128]{1,0:T(8,128)(2,1)} %refs_5_.1, bf16[128,128]{1,0:T(8,128)(2,1)} %refs_6_.1, ...), custom_call_target="tpu_custom_call" | custom-call | tf_op jit(solution)/shard_map/pallas_call | solution.py:546
  129.2 1.2 copy.12
